TPU v7x, 128 devices: a whole 4x4x4 slice. The times are simulated.
128 devices in a mesh: row: 8 (over x, core), col: 16 (over y, z).
Axes of the slice: x: 4, y: 4, z: 4, core: 2. Of those that a mesh axis runs over, the one named last changes fastest.
Arguments:
- momentum: float32 [8192, 28672], P('row', 'col'), may hold values from -200 to 200
- gradient: bfloat16 [8192, 28672], P('row', 'col'), may hold values from -6 to 6
- weight: bfloat16 [8192, 28672], P('row', 'col'), may hold values from -6 to 6
- basis_prev: float32 [8192, 512], P('row'), may hold values from -0.0625 to 0.0625
Outputs:
- new_momentum: float32 [8192, 28672], P('row', 'col')
- new_basis: float32 [8192, 512], P('row')
- new_weight: bfloat16 [8192, 28672], P('row', 'col')
All inputs are finite; a program needn't handle non-finite values.
Results may differ from a plain program's by a relative error of at most 0.001.
Values sent between devices are 32-bit elements; how exact they have to be, the bound alone decides.
No kernel may reach another device: no remote copies, remote signals or barrier semaphores. Data moves between devices by JAX's collectives and lax.ppermute only.
A program may use at most 128 MiB of HBM per device.

v0:
```python
import math

import jax
import jax.numpy as jnp
from jax import lax
from jax.experimental import pallas as pl
from jax.experimental.pallas import tpu as pltpu
from jax.sharding import PartitionSpec as P

D = 8192
FF = 28672
RANK = 512

decay_keep = 0.95
step_rms = 0.2
norm_eps = 1e-06
highest = lax.Precision.HIGHEST
high = lax.Precision.HIGH
block = 128


def dot(first, second, dims, precision):
    return lax.dot_general(
        first, second, ((dims[:1], dims[1:]), ((), ())), precision=precision, preferred_element_type=jnp.float32
    )


other_core = [(i, i ^ 1) for i in range(8)]


def along_x(shift):
    return [(2 * x + core, 2 * ((x + shift) % 4) + core) for x in range(4) for core in range(2)]


def along_y(shift):
    return [(4 * y + z, 4 * ((y + shift) % 4) + z) for y in range(4) for z in range(4)]


def along_z(shift):
    return [(4 * y + z, 4 * y + (z + shift) % 4) for y in range(4) for z in range(4)]


def pick(array, index, size):
    return lax.dynamic_slice_in_dim(array, index * size, size, 0)


def total(own, got):
    return (own + got[1]) + (got[0] + got[2])


def ring_sum(array, axis, moves):
    return total(array, [lax.ppermute(array, axis, moves(s)) for s in (1, 2, 3)])


def ring_scatter(array, axis, place, moves):
    size = array.shape[0] // 4
    got = [lax.ppermute(pick(array, (place + s) % 4, size), axis, moves(s)) for s in (1, 2, 3)]
    return total(pick(array, place, size), got)


def ring_gather(array, axis, place, moves):
    size = array.shape[0]
    parts = [array] + [lax.ppermute(array, axis, moves(s)) for s in (1, 2, 3)]
    whole = jnp.zeros((4 * size,) + array.shape[1:], array.dtype)
    for s, part in enumerate(parts):
        whole = lax.dynamic_update_slice_in_dim(whole, part, (place - s) % 4 * size, 0)
    return whole


def core_scatter(array, core):
    half = array.shape[0] // 2
    return pick(array, core, half) + lax.ppermute(pick(array, 1 - core, half), "row", other_core)


def core_gather(array, core):
    half = array.shape[0]
    whole = jnp.zeros((2 * half,) + array.shape[1:], array.dtype)
    whole = lax.dynamic_update_slice_in_dim(whole, array, core * half, 0)
    return lax.dynamic_update_slice_in_dim(whole, lax.ppermute(array, "row", other_core), (1 - core) * half, 0)


def ring_parts(array, moves):
    return [array] + [lax.ppermute(array, "row", moves(s)) for s in (1, 2, 3)]


def invert_factor(square):
    size = square.shape[0]
    rows = lax.broadcasted_iota(jnp.int32, (8, size), 0)
    down = lax.broadcasted_iota(jnp.int32, (size, size), 0)
    across = lax.broadcasted_iota(jnp.int32, (size, size), 1)
    rest, image, done = square, jnp.where(down == across, 1.0, 0.0).astype(jnp.float32), []
    for first in range(0, size, 8):
        count = size - first
        cols = [jnp.broadcast_to(rest[:, first + j : first + j + 1], (count, size)) for j in range(8)]
        top, top_image = rest[:8], image[:8]
        rest, image = rest[8:], image[8:]
        for k in range(8):
            scale = lax.rsqrt(cols[k][k : k + 1, :])
            col = cols[k] * scale
            row, row_image = top[k : k + 1, :] * scale, top_image[k : k + 1, :] * scale
            top_image = jnp.where(rows == k, row_image, top_image)
            below = jnp.where(rows > k, col[:8], 0.0)
            top = top - below * row
            top_image = top_image - below * row_image
            if count > 8:
                rest = rest - col[8:] * row
                image = image - col[8:] * row_image
            for j in range(k + 1, 8):
                cols[j] = cols[j] - col * col[j : j + 1, :]
        done.append(top_image)
    return jnp.concatenate(done, axis=0)


def inverse_kernel(gram_ref, out_ref, left_ref, image_ref):
    left_ref[...] = gram_ref[...]
    image_ref[...] = jnp.zeros_like(image_ref)
    out_ref[...] = jnp.zeros_like(out_ref)
    for low in range(0, RANK, block):
        top = low + block
        corner = invert_factor(left_ref[low:top, low:top])
        out_ref[low:top, low:top] = corner
        if low:
            out_ref[low:top, :low] = dot(corner, image_ref[low:top, :low], (1, 0), highest)
        if top < RANK:
            panel = dot(left_ref[top:, low:top], corner, (1, 1), highest)
            for at in range(top, RANK, block):
                part = panel[at - top :]
                left_ref[at:, at : at + block] -= dot(part, part[:block], (1, 1), highest)
            image_ref[top:, :top] -= dot(panel, out_ref[low:top, :top], (1, 0), highest)


def inverse_of_factor(gram_sum):
    square = jax.ShapeDtypeStruct((RANK, RANK), jnp.float32)
    return pl.pallas_call(
        inverse_kernel,
        out_shape=square,
        scratch_shapes=[pltpu.VMEM((RANK, RANK), jnp.float32)] * 2,
        compiler_params=pltpu.CompilerParams(vmem_limit_bytes=32 * 2**20),
        cost_estimate=pl.CostEstimate(flops=2 * RANK**3, bytes_accessed=8 * RANK**2, transcendentals=RANK),
        name="inverse_of_factor",
    )(gram_sum)


def exchange(array):
    return lax.all_to_all(array, "col", 0, 0)


def col_scatter(array):
    return jnp.sum(exchange(array.reshape((16, array.shape[0] // 16) + array.shape[1:])), axis=0)


def col_gather(array):
    return exchange(jnp.broadcast_to(array[None], (16,) + array.shape)).reshape((16 * array.shape[0],) + array.shape[1:])


def split(array):
    high_part = array.astype(jnp.bfloat16)
    return high_part, (array - high_part.astype(jnp.float32)).astype(jnp.bfloat16)


def dot16(first, second, dims):
    return lax.dot_general(first, second, ((dims[:1], dims[1:]), ((), ())), preferred_element_type=jnp.float32)


def dot_split(first, second, dims):
    return dot16(first[0], second[0], dims) + (dot16(first[0], second[1], dims) + dot16(first[1], second[0], dims))


def call(kernel, grid, in_specs, out_specs, out_shape, scratch, flops, moved, name, room):
    return pl.pallas_call(
        kernel,
        grid=grid,
        in_specs=in_specs,
        out_specs=out_specs,
        out_shape=out_shape,
        scratch_shapes=scratch,
        compiler_params=pltpu.CompilerParams(vmem_limit_bytes=room * 2**20),
        cost_estimate=pl.CostEstimate(flops=flops, bytes_accessed=moved, transcendentals=0),
        name=name,
    )


def tall(rows, columns):
    return pl.BlockSpec((rows, columns), lambda i: (i, 0))


def whole(*shape):
    return pl.BlockSpec(shape, lambda i: (0,) * len(shape), pipeline_mode=pl.Buffered(1))


def left_kernel(half_ref, momentum_ref, gradient_ref, basis_ref, left_ref):
    blended = split(momentum_ref[...] + gradient_ref[...].astype(jnp.float32))
    part = dot_split(blended, split(basis_ref[...]), (0, 0))

    @pl.when(pl.program_id(0) == 0)
    def _():
        left_ref[...] = part

    @pl.when(pl.program_id(0) > 0)
    def _():
        left_ref[...] += part


def left_half(half, momentum, gradient, basis_prev):
    rows, columns = momentum.shape
    tile, width = 512, columns // 2
    piece = pl.BlockSpec((tile, width), lambda i, half: (i, half[0]))
    return pl.pallas_call(
        left_kernel,
        grid_spec=pltpu.PrefetchScalarGridSpec(
            num_scalar_prefetch=1,
            grid=(rows // tile,),
            in_specs=[piece, piece, pl.BlockSpec((tile, RANK), lambda i, half: (i, 0))],
            out_specs=pl.BlockSpec((width, RANK), lambda i, half: (0, 0)),
        ),
        out_shape=jax.ShapeDtypeStruct((width, RANK), jnp.float32),
        compiler_params=pltpu.CompilerParams(vmem_limit_bytes=54 * 2**20),
        cost_estimate=pl.CostEstimate(
            flops=6 * rows * width * RANK, bytes_accessed=6 * rows * width + 8 * width * RANK, transcendentals=0
        ),
        name="left_half",
    )(half, momentum, gradient, basis_prev)


def product_kernel(place_ref, momentum_ref, gradient_ref, *refs):
    parts, (product_ref, left_ref, high_ref, low_ref) = refs[:8], refs[8:]

    @pl.when(pl.program_id(0) == 0)
    def _():
        x, core = place_ref[0], place_ref[1]
        for i, part in enumerate(parts):
            at = 4 * (core if i < 4 else 1 - core) + (x + 4 - i % 4) % 4
            value = part[...]
            left_ref[at] = value
            high_ref[at], low_ref[at] = split(value)

    count = left_ref.shape[0] * left_ref.shape[1]
    left = [ref[...].reshape(count, RANK) for ref in (high_ref, low_ref)]
    blended = split(momentum_ref[...] + gradient_ref[...].astype(jnp.float32))
    product_ref[...] = dot_split(blended, left, (1, 0))


def blended_times_left(place, momentum, gradient, parts):
    rows, columns = momentum.shape
    tile, size = 256, parts[0].shape[0]
    shape = (8, size, RANK)
    return call(
        product_kernel,
        (rows // tile,),
        [pl.BlockSpec(memory_space=pltpu.SMEM), tall(tile, columns), tall(tile, columns)] + [whole(size, RANK)] * 8,
        [tall(tile, RANK), whole(*shape)],
        [jax.ShapeDtypeStruct((rows, RANK), jnp.float32), jax.ShapeDtypeStruct(shape, jnp.float32)],
        [pltpu.VMEM(shape, jnp.bfloat16)] * 2,
        6 * rows * columns * RANK,
        6 * rows * columns + 8 * columns * RANK,
        "blended_times_left",
        48,
    )(place, momentum, gradient, *parts)


def ortho_kernel(left_ref, inverse_ref, high_ref, low_ref, inverse_high_ref, inverse_low_ref):
    @pl.when(pl.program_id(0) == 0)
    def _():
        inverse_high_ref[...], inverse_low_ref[...] = split(inverse_ref[...])

    inverse = inverse_high_ref[...], inverse_low_ref[...]
    high_ref[...], low_ref[...] = split(dot_split(inverse, split(left_ref[...]), (1, 1)))


def ortho_halves(left_full, inverse):
    columns, tile = left_full.shape[0], 256
    return call(
        ortho_kernel,
        (columns // tile,),
        [tall(tile, RANK), whole(RANK, RANK)],
        [pl.BlockSpec((RANK, tile), lambda i: (0, i))] * 2,
        [jax.ShapeDtypeStruct((RANK, columns), jnp.bfloat16)] * 2,
        [pltpu.VMEM((RANK, RANK), jnp.bfloat16)] * 2,
        6 * columns * RANK**2,
        8 * columns * RANK,
        "ortho_halves",
        12,
    )(left_full, inverse)


def right_kernel(product_ref, inverse_ref, right_ref, squares_ref, inverse_high_ref, inverse_low_ref):
    @pl.when(pl.program_id(0) == 0)
    def _():
        inverse_high_ref[...], inverse_low_ref[...] = split(inverse_ref[...])
        squares_ref[...] = jnp.zeros_like(squares_ref)

    right = dot_split(split(product_ref[...]), (inverse_high_ref[...], inverse_low_ref[...]), (1, 1))
    right_ref[...] = right
    squares_ref[...] += jnp.sum(right * right, axis=0, keepdims=True)


def right_and_squares(product_full, inverse):
    rows, tile = product_full.shape[0], 256
    return call(
        right_kernel,
        (rows // tile,),
        [tall(tile, RANK), whole(RANK, RANK)],
        [tall(tile, RANK), whole(1, RANK)],
        [jax.ShapeDtypeStruct((rows, RANK), jnp.float32), jax.ShapeDtypeStruct((1, RANK), jnp.float32)],
        [pltpu.VMEM((RANK, RANK), jnp.bfloat16)] * 2,
        6 * rows * RANK**2,
        8 * rows * RANK,
        "right_and_squares",
        12,
    )(product_full, inverse)


def momentum_kernel(right_ref, ortho_ref, momentum_ref, gradient_ref, out_ref):
    projection = dot16(right_ref[...].astype(jnp.bfloat16), ortho_ref[...], (1, 0))
    out_ref[...] = momentum_ref[...] + gradient_ref[...].astype(jnp.float32) - (1.0 - decay_keep) * projection


def next_momentum(right_full, ortho_high, momentum, gradient):
    rows, columns = momentum.shape
    tile = 256
    return call(
        momentum_kernel,
        (rows // tile,),
        [tall(tile, RANK), whole(RANK, columns), tall(tile, columns), tall(tile, columns)],
        tall(tile, columns),
        jax.ShapeDtypeStruct((rows, columns), jnp.float32),
        [],
        2 * rows * columns * RANK,
        10 * rows * columns,
        "next_momentum",
        20,
    )(right_full, ortho_high, momentum, gradient)


def weight_kernel(right_ref, squares_ref, high_ref, low_ref, weight_ref, basis_ref, out_ref):
    basis = right_ref[...] / jnp.sqrt(squares_ref[...] + norm_eps)
    basis_ref[...] = basis
    update = dot_split(split(basis), (high_ref[...], low_ref[...]), (1, 0))
    scale_step = step_rms * math.sqrt(D * FF / RANK)
    out_ref[...] = (weight_ref[...].astype(jnp.float32) - scale_step * update).astype(jnp.bfloat16)


def next_weight(right_full, squares, ortho, weight):
    rows, columns = weight.shape
    tile = 256
    return call(
        weight_kernel,
        (rows // tile,),
        [tall(tile, RANK), whole(1, RANK), whole(RANK, columns), whole(RANK, columns), tall(tile, columns)],
        [tall(tile, RANK), tall(tile, columns)],
        [jax.ShapeDtypeStruct((rows, RANK), jnp.float32), jax.ShapeDtypeStruct((rows, columns), jnp.bfloat16)],
        [],
        6 * rows * columns * RANK,
        4 * rows * columns + 8 * rows * RANK,
        "next_weight",
        24,
    )(right_full, squares, *ortho, weight)


def exchange(array):
    return lax.all_to_all(array, "col", 0, 0)


def col_scatter(array):
    return jnp.sum(exchange(array.reshape((16, array.shape[0] // 16) + array.shape[1:])), axis=0)


def col_gather(array):
    return exchange(jnp.broadcast_to(array[None], (16,) + array.shape)).reshape((16 * array.shape[0],) + array.shape[1:])


def on_device(momentum, gradient, weight, basis_prev):
    row, col = lax.axis_index("row"), lax.axis_index("col")
    x, core, y, z = row // 2, row % 2, col // 4, col % 4
    given = left_half(jnp.reshape(1 - core, (1,)).astype(jnp.int32), momentum, gradient, basis_prev)
    taken = lax.ppermute(given, "row", other_core)
    kept = left_half(jnp.reshape(core, (1,)).astype(jnp.int32), momentum, gradient, basis_prev)
    left_rows = ring_scatter(kept + taken, "row", x, along_x)

    parts = ring_parts(left_rows, along_x)
    gram_rows = core_scatter(dot(left_rows, left_rows, (0, 0), highest), core)
    gram_rows = ring_scatter(ring_scatter(gram_rows, "col", y, along_y), "col", z, along_z)
    parts, gram_rows = lax.optimization_barrier((parts, gram_rows))
    parts = parts + [lax.ppermute(part, "row", other_core) for part in parts]
    place = jnp.stack([x, core]).astype(jnp.int32)
    product, left_full = blended_times_left(place, momentum, gradient, parts)
    left_full = left_full.reshape(-1, RANK)
    got = ring_parts(gram_rows, along_x)
    product, got = lax.optimization_barrier((product, got))
    gram_rows = total(got[0], got[1:])

    count = gram_rows.shape[0]
    gram_copies = jnp.broadcast_to(gram_rows[None], (16,) + gram_rows.shape)
    mixed = exchange(jnp.concatenate([gram_copies, product.reshape(16, -1, RANK)], 1))
    product_full = col_gather(jnp.sum(mixed[:, count:], axis=0))
    inverse = inverse_of_factor(core_gather(mixed[:, :count].reshape(-1, RANK), core))
    ortho = ortho_halves(left_full, inverse)
    ortho, product_full = lax.optimization_barrier((ortho, product_full))

    right_full, squares = right_and_squares(product_full, inverse)
    squares = squares + lax.ppermute(squares, "row", other_core)
    squares = ring_sum(squares, "row", along_x)
    new_momentum = next_momentum(right_full, ortho[0], momentum, gradient)
    new_basis, new_weight = next_weight(right_full, squares, ortho, weight)
    return (new_momentum, new_basis, new_weight)


def solution(mesh):
    return jax.shard_map(
        on_device,
        mesh=mesh,
        in_specs=(P("row", "col"), P("row", "col"), P("row", "col"), P("row", None)),
        out_specs=(P("row", "col"), P("row", None), P("row", "col")),
        check_vma=False,
    )
```

profile of v0, /device:TPU:1, one launch (start us, length us, event | category | flops | bytes accessed | tf_op | source)
XLA Modules:
  0.0 193.4 jit_solution(3976608360143680731)
XLA Ops:
  0.6 6.9 %left_half.3 = f32[896,512]{1,0:T(8,128)} custom-call(s32[1]{0:T(128)} %bitcast.2.half_ref, f32[1024,1792]{1,0:T(8,128)} %momentum_ref.7, bf16[1024,1792]{1,0:T(8,128)(2,1)} %gradient_ref.7, f32[1024,512]{1,0:T(8,128)} %basis_ref.3), custom_call_target="tpu_custom_call" | custom-call | flops 2818572288 | bytes 9175040 | tf_op jit(solution)/shard_map/left_half/pallas_call | solution.py:208
  7.5 1.4 collective-permute-start
  8.9 6.9 %left_half.2 = f32[896,512]{1,0:T(8,128)} custom-call(s32[1]{0:T(128)} %bitcast.1.half_ref, f32[1024,1792]{1,0:T(8,128)} %momentum_ref.7, bf16[1024,1792]{1,0:T(8,128)(2,1)} %gradient_ref.7, f32[1024,512]{1,0:T(8,128)} %basis_ref.3), custom_call_target="tpu_custom_call" | custom-call | flops 2818572288 | bytes 9175040 | tf_op jit(solution)/shard_map/left_half/pallas_call | solution.py:208
  15.8 2.5 %add.162 = f32[896,512]{1,0:T(8,128)S(1)} add(f32[896,512]{1,0:T(8,128)} %left_half.2, f32[896,512]{1,0:T(8,128)} %collective-permute-done) | non-fusion elementwise | flops 458752 | bytes 5505024 | tf_op jit(solution)/shard_map/add | solution.py:378
  18.3 1.1 constant_dynamic-slice_fusion.9
  19.3 2.8 %collective-permute-start.1 = (f32[224,512]{1,0:T(8,128)}, f32[224,512]{1,0:T(8,128)S(1)}, u32[]{:S(2)}, u32[]{:S(2)}) collective-permute-start(f32[224,512]{1,0:T(8,128)} %get-tuple-element.45), channel_id=1, source_target_pairs={{0,64},{16,80},{32,96},{48,112},{64,0},{80,16},{96,32},{112,48},{1... | collective-permute-start | bytes 1376264 | tf_op jit(solution)/shard_map/ppermute | solution.py:57
  22.2 0.8 collective-permute-start.3
  23.0 0.6 collective-permute-start.2
  23.6 9.6 %collective-permute-done.1 = f32[224,512]{1,0:T(8,128)S(1)} collective-permute-done((f32[224,512]{1,0:T(8,128)}, f32[224,512]{1,0:T(8,128)S(1)}, u32[]{:S(2)}, u32[]{:S(2)}) %collective-permute-start.1) | collective-permute-done | bytes 458784 | tf_op jit(solution)/shard_map/ppermute | solution.py:57
  33.2 10.1 %collective-permute-done.3 = f32[224,512]{1,0:T(8,128)S(1)} collective-permute-done((f32[224,512]{1,0:T(8,128)}, f32[224,512]{1,0:T(8,128)S(1)}, u32[]{:S(2)}, u32[]{:S(2)}) %collective-permute-start.3) | collective-permute-done | bytes 458784 | tf_op jit(solution)/shard_map/ppermute | solution.py:57
  43.4 0.0 collective-permute-done.2
  43.4 1.2 add_add_fusion.refs_0_
  44.6 1.1 fusion
  45.8 0.7 collective-permute-start.7
  46.5 1.5 collective-permute-done.7
  48.1 0.1 dynamic-slice_add_fusion
  48.2 3.0 %collective-permute-start.8 = (f32[64,512]{1,0:T(8,128)S(1)}, f32[64,512]{1,0:T(8,128)S(1)}, u32[]{:S(2)}, u32[]{:S(2)}) collective-permute-start(f32[64,512]{1,0:T(8,128)S(1)} %get-tuple-element.48), channel_id=1, source_target_pairs={{0,8},{1,9},{2,10},{3,11},{4,12},{5,13},{6,14},{7,15},{8,0},{9,1},... | collective-permute-start | bytes 393224 | tf_op jit(solution)/shard_map/ppermute | solution.py:57
  51.2 0.8 collective-permute-start.10
  51.9 0.7 collective-permute-start.9
  52.6 2.3 %collective-permute-start.6 = (f32[224,512]{1,0:T(8,128)S(1)}, f32[224,512]{1,0:T(8,128)S(1)}, u32[]{:S(2)}, u32[]{:S(2)}) collective-permute-start(f32[224,512]{1,0:T(8,128)S(1)} %add_add_fusion.refs_0_), channel_id=1, source_target_pairs={{0,96},{16,112},{32,0},{48,16},{64,32},{80,48},{96,64},{112,80},{1... | collective-permute-start | bytes 1376264 | tf_op jit(solution)/shard_map/ppermute | solution.py:83
  55.0 0.7 collective-permute-start.5
  55.7 0.5 collective-permute-start.4
  56.2 1.4 collective-permute-done.10
  57.7 3.7 %collective-permute-start.11 = (f32[16,512]{1,0:T(8,128)S(1)}, f32[16,512]{1,0:T(8,128)S(1)}, u32[]{:S(2)}, u32[]{:S(2)}) collective-permute-start(f32[16,512]{1,0:T(8,128)S(1)} %get-tuple-element.51), channel_id=1, source_target_pairs={{0,2},{1,3},{2,0},{3,1},{4,6},{5,7},{6,4},{7,5},{8,10},{9,11},{10,... | collective-permute-start | bytes 98312 | tf_op jit(solution)/shard_map/ppermute | solution.py:57
  61.3 0.4 collective-permute-start.13
  61.8 1.2 collective-permute-done.11
  62.9 1.0 collective-permute-start.12
  63.9 0.5 collective-permute-done.13
  64.4 3.3 %collective-permute-done.12 = f32[16,512]{1,0:T(8,128)S(1)} collective-permute-done((f32[16,512]{1,0:T(8,128)S(1)}, f32[16,512]{1,0:T(8,128)S(1)}, u32[]{:S(2)}, u32[]{:S(2)}) %collective-permute-start.12) | collective-permute-done | bytes 32800 | tf_op jit(solution)/shard_map/ppermute | solution.py:57
  67.7 11.0 %collective-permute-done.4.refs_1_ = f32[224,512]{1,0:T(8,128)S(1)} collective-permute-done((f32[224,512]{1,0:T(8,128)S(1)}, f32[224,512]{1,0:T(8,128)S(1)}, u32[]{:S(2)}, u32[]{:S(2)}) %collective-permute-start.4) | collective-permute-done | bytes 458784 | tf_op jit(solution)/shard_map/ppermute | solution.py:83
  78.8 0.5 collective-permute-start.14
  79.3 0.0 collective-permute-start.15
  79.3 0.5 collective-permute-start.16
  79.8 0.1 pad_add_fusion.place_ref
  79.9 0.3 collective-permute-start.20
  80.2 0.5 collective-permute-done.14.refs_4_
  80.7 0.7 collective-permute-start.19
  81.4 0.2 collective-permute-start.18
  81.6 0.4 collective-permute-done.16.refs_6_
  82.0 0.7 collective-permute-done.17.refs_7_
  82.7 10.0 %blended_times_left.1 = (f32[1024,512]{1,0:T(8,128)S(1)}, f32[8,224,512]{2,1,0:T(8,128)}) custom-call(s32[2]{0:T(128)S(1)} %pad_add_fusion.place_ref, f32[1024,1792]{1,0:T(8,128)} %momentum_ref.7, bf16[1024,1792]{1,0:T(8,128)(2,1)} %gradient_ref.7, f32[224,512]{1,0:T(8,128)S(1)} %add_add_fusion.refs_0_, f32[224,512]{1,0:T(8,128)S(1)} %collective-permute-done.4.refs_1_, ...), custom_call_target="tpu_custom_call" | custom-call | flops 5637144576 | bytes 18350080 | tf_op jit(solution)/shard_map/blended_times_left/pallas_call | solution.py:247
  92.7 0.1 broadcast_in_dim.7
  92.7 0.3 pad_maximum_fusion
  93.0 39.5 %all_to_all.10 = f32[16,80,512]{2,1,0:T(8,128)} all-to-all(f32[16,80,512]{2,1,0:T(8,128)S(1)} %pad_maximum_fusion), channel_id=1, replica_groups=mesh['row'=8,'col'=16] {'col'}, dimensions={0} | all-to-all | bytes 5242880 | tf_op jit(solution)/shard_map/all_to_all | solution.py:361
  132.5 1.8 slice_reduce_fusion
  134.3 1.6 broadcast_in_dim.8
  135.9 3.7 %all-to-all-start.1 = ((f32[16,64,512]{2,1,0:T(8,128)}), f32[16,64,512]{2,1,0:T(8,128)S(1)}, u32[]{:S(2)}, u32[]{:S(2)}) async-start(f32[16,64,512]{2,1,0:T(8,128)} %broadcast_in_dim.8), calls=%async_computation.1 | async-start | bytes 4194304 | tf_op jit(solution)/shard_map/all_to_all | solution.py:361
  139.6 1.1 slice.8
  140.7 2.4 %collective-permute-start.21 = (f32[256,512]{1,0:T(8,128)S(1)}, f32[256,512]{1,0:T(8,128)S(1)}, u32[]{:S(2)}, u32[]{:S(2)}) collective-permute-start(f32[256,512]{1,0:T(8,128)S(1)} %bitcast.12), channel_id=1, source_target_pairs={{0,16},{16,0},{32,48},{48,32},{64,80},{80,64},{96,112},{112,96},{1... | collective-permute-start | bytes 1572872 | tf_op jit(solution)/shard_map/ppermute | solution.py:79
  143.1 0.1 broadcast_in_dim.6
  143.3 1.4 collective-permute-done.21
  144.7 18.4 %inverse_of_factor.1.inverse_ref = f32[512,512]{1,0:T(8,128)S(1)} custom-call(f32[512,512]{1,0:T(8,128)S(1)} %constant_dynamic-update-slice_fusion.gram_ref), custom_call_target="tpu_custom_call" | custom-call | flops 268435456 | bytes 2097152 | tf_op jit(solution)/shard_map/inverse_of_factor/pallas_call | solution.py:134
  163.1 4.7 %ortho_halves.1 = (bf16[512,1792]{1,0:T(8,128)(2,1)S(1)}, bf16[512,1792]{1,0:T(8,128)(2,1)S(1)}) custom-call(f32[1792,512]{1,0:T(8,128)S(1)} %bitcast.11, f32[512,512]{1,0:T(8,128)S(1)} %inverse_of_factor.1.inverse_ref), custom_call_target="tpu_custom_call" | custom-call | flops 2818572288 | bytes 7340032 | tf_op jit(solution)/shard_map/ortho_halves/pallas_call | solution.py:272
  167.9 1.2 copy-done.2
  169.1 1.3 copy-done.6
  170.4 2.7 %right_and_squares.1 = (f32[1024,512]{1,0:T(8,128)S(1)}, f32[1,512]{1,0:T(1,128)S(1)}) custom-call(f32[1024,512]{1,0:T(8,128)S(1)} %bitcast.9, f32[512,512]{1,0:T(8,128)S(1)} %inverse_of_factor.1.inverse_ref), custom_call_target="tpu_custom_call" | custom-call | flops 1610612736 | bytes 4194304 | tf_op jit(solution)/shard_map/right_and_squares/pallas_call | solution.py:299
  173.0 0.5 collective-permute-start.22
  173.5 0.8 collective-permute-done.22
  174.3 1.5 collective-permute-start.25
  175.8 2.3 %collective-permute-start.23 = (f32[1,512]{1,0:T(1,128)S(1)}, f32[1,512]{1,0:T(1,128)S(1)}, u32[]{:S(2)}, u32[]{:S(2)}) collective-permute-start(f32[1,512]{1,0:T(1,128)S(1)} %add.209), channel_id=1, source_target_pairs={{0,64},{16,80},{32,96},{48,112},{64,0},{80,16},{96,32},{112,48},{1... | collective-permute-start | bytes 6152 | tf_op jit(solution)/shard_map/ppermute | solution.py:52
  178.0 3.1 %copy-done = f32[1024,1792]{1,0:T(8,128)S(1)} copy-done((f32[1024,1792]{1,0:T(8,128)S(1)}, f32[1024,1792]{1,0:T(8,128)}, u32[]{:S(2)}) %copy-start) | copy-done | bytes 7340056
  181.1 4.4 %next_momentum.1 = f32[1024,1792]{1,0:T(8,128)} custom-call(f32[1024,512]{1,0:T(8,128)S(1)} %get-tuple-element.39.right_ref, bf16[512,1792]{1,0:T(8,128)(2,1)S(1)} %copy-done.3, f32[1024,1792]{1,0:T(8,128)S(1)} %copy-done, bf16[1024,1792]{1,0:T(8,128)(2,1)S(1)} %copy-done.1), custom_call_target="tpu_custom_call" | custom-call | flops 1879048192 | bytes 18350080 | tf_op jit(solution)/shard_map/next_momentum/pallas_call | solution.py:321
  185.6 0.5 copy-done.7
  186.1 7.4 %next_weight.1 = (f32[1024,512]{1,0:T(8,128)}, bf16[1024,1792]{1,0:T(8,128)(2,1)}) custom-call(f32[1024,512]{1,0:T(8,128)S(1)} %get-tuple-element.39.right_ref, f32[1,512]{1,0:T(1,128)S(1)} %add_add_fusion.4.squares_ref, bf16[512,1792]{1,0:T(8,128)(2,1)S(1)} %copy-done.3, bf16[512,1792]{1,0:T(8,128)(2,1)S(1)} %copy-done.7, bf16[1024,1792]{1,0:T(8,128)(2,1)S(1)} %copy-done.4), custom_call_target="tpu_custom_call" | custom-call | flops 5637144576 | bytes 11534336 | tf_op jit(solution)/shard_map/next_weight/pallas_call | solution.py:346
  (37 shorter events, 0.3 us)
Async XLA Ops:
  7.5 8.3 %collective-permute-start = (f32[896,512]{1,0:T(8,128)}, f32[896,512]{1,0:T(8,128)}, u32[]{:S(2)}, u32[]{:S(2)}) collective-permute-start(f32[896,512]{1,0:T(8,128)} %left_half.3), channel_id=1, source_target_pairs={{0,16},{16,0},{32,48},{48,32},{64,80},{80,64},{96,112},{112,96},{1... | collective-permute-start | bytes 5505032 | tf_op jit(solution)/shard_map/ppermute | solution.py:376
  19.3 13.9 %collective-permute-start.1 = (f32[224,512]{1,0:T(8,128)}, f32[224,512]{1,0:T(8,128)S(1)}, u32[]{:S(2)}, u32[]{:S(2)}) collective-permute-start(f32[224,512]{1,0:T(8,128)} %get-tuple-element.45), channel_id=1, source_target_pairs={{0,64},{16,80},{32,96},{48,112},{64,0},{80,16},{96,32},{112,48},{1... | collective-permute-start | bytes 1376264 | tf_op jit(solution)/shard_map/ppermute | solution.py:57
  22.2 21.2 %collective-permute-start.3 = (f32[224,512]{1,0:T(8,128)}, f32[224,512]{1,0:T(8,128)S(1)}, u32[]{:S(2)}, u32[]{:S(2)}) collective-permute-start(f32[224,512]{1,0:T(8,128)} %get-tuple-element.46), channel_id=1, source_target_pairs={{0,96},{16,112},{32,0},{48,16},{64,32},{80,48},{96,64},{112,80},{1... | collective-permute-start | bytes 1376264 | tf_op jit(solution)/shard_map/ppermute | solution.py:57
  23.0 20.4 %collective-permute-start.2 = (f32[224,512]{1,0:T(8,128)S(1)}, f32[224,512]{1,0:T(8,128)}, u32[]{:S(2)}, u32[]{:S(2)}) collective-permute-start(f32[224,512]{1,0:T(8,128)S(1)} %get-tuple-element.47), channel_id=1, source_target_pairs={{0,32},{16,48},{32,64},{48,80},{64,96},{80,112},{96,0},{112,16},{1... | collective-permute-start | bytes 1376264 | tf_op jit(solution)/shard_map/ppermute | solution.py:57
  45.8 2.3 %collective-permute-start.7 = (f32[256,512]{1,0:T(8,128)S(1)}, f32[256,512]{1,0:T(8,128)S(1)}, u32[]{:S(2)}, u32[]{:S(2)}) collective-permute-start(f32[256,512]{1,0:T(8,128)S(1)} %constant_dynamic-slice_fusion.6), channel_id=1, source_target_pairs={{0,16},{16,0},{32,48},{48,32},{64,80},{80,64},{96,112},{112,96},{1... | collective-permute-start | bytes 1572872 | tf_op jit(solution)/shard_map/ppermute | solution.py:72
  48.2 7.5 %collective-permute-start.8 = (f32[64,512]{1,0:T(8,128)S(1)}, f32[64,512]{1,0:T(8,128)S(1)}, u32[]{:S(2)}, u32[]{:S(2)}) collective-permute-start(f32[64,512]{1,0:T(8,128)S(1)} %get-tuple-element.48), channel_id=1, source_target_pairs={{0,8},{1,9},{2,10},{3,11},{4,12},{5,13},{6,14},{7,15},{8,0},{9,1},... | collective-permute-start | bytes 393224 | tf_op jit(solution)/shard_map/ppermute | solution.py:57
  51.2 6.5 %collective-permute-start.10 = (f32[64,512]{1,0:T(8,128)S(1)}, f32[64,512]{1,0:T(8,128)S(1)}, u32[]{:S(2)}, u32[]{:S(2)}) collective-permute-start(f32[64,512]{1,0:T(8,128)S(1)} %get-tuple-element.49), channel_id=1, source_target_pairs={{0,12},{1,13},{2,14},{3,15},{4,0},{5,1},{6,2},{7,3},{8,4},{9,5},{1... | collective-permute-start | bytes 393224 | tf_op jit(solution)/shard_map/ppermute | solution.py:57
  51.9 5.7 %collective-permute-start.9 = (f32[64,512]{1,0:T(8,128)S(1)}, f32[64,512]{1,0:T(8,128)S(1)}, u32[]{:S(2)}, u32[]{:S(2)}) collective-permute-start(f32[64,512]{1,0:T(8,128)S(1)} %get-tuple-element.50), channel_id=1, source_target_pairs={{0,4},{1,5},{2,6},{3,7},{4,8},{5,9},{6,10},{7,11},{8,12},{9,13},{1... | collective-permute-start | bytes 393224 | tf_op jit(solution)/shard_map/ppermute | solution.py:57
  52.6 15.1 %collective-permute-start.6 = (f32[224,512]{1,0:T(8,128)S(1)}, f32[224,512]{1,0:T(8,128)S(1)}, u32[]{:S(2)}, u32[]{:S(2)}) collective-permute-start(f32[224,512]{1,0:T(8,128)S(1)} %add_add_fusion.refs_0_), channel_id=1, source_target_pairs={{0,96},{16,112},{32,0},{48,16},{64,32},{80,48},{96,64},{112,80},{1... | collective-permute-start | bytes 1376264 | tf_op jit(solution)/shard_map/ppermute | solution.py:83
  55.0 12.7 %collective-permute-start.5 = (f32[224,512]{1,0:T(8,128)S(1)}, f32[224,512]{1,0:T(8,128)S(1)}, u32[]{:S(2)}, u32[]{:S(2)}) collective-permute-start(f32[224,512]{1,0:T(8,128)S(1)} %add_add_fusion.refs_0_), channel_id=1, source_target_pairs={{0,64},{16,80},{32,96},{48,112},{64,0},{80,16},{96,32},{112,48},{1... | collective-permute-start | bytes 1376264 | tf_op jit(solution)/shard_map/ppermute | solution.py:83
  55.7 23.1 %collective-permute-start.4 = (f32[224,512]{1,0:T(8,128)S(1)}, f32[224,512]{1,0:T(8,128)S(1)}, u32[]{:S(2)}, u32[]{:S(2)}) collective-permute-start(f32[224,512]{1,0:T(8,128)S(1)} %add_add_fusion.refs_0_), channel_id=1, source_target_pairs={{0,32},{16,48},{32,64},{48,80},{64,96},{80,112},{96,0},{112,16},{1... | collective-permute-start | bytes 1376264 | tf_op jit(solution)/shard_map/ppermute | solution.py:83
  57.7 5.3 %collective-permute-start.11 = (f32[16,512]{1,0:T(8,128)S(1)}, f32[16,512]{1,0:T(8,128)S(1)}, u32[]{:S(2)}, u32[]{:S(2)}) collective-permute-start(f32[16,512]{1,0:T(8,128)S(1)} %get-tuple-element.51), channel_id=1, source_target_pairs={{0,2},{1,3},{2,0},{3,1},{4,6},{5,7},{6,4},{7,5},{8,10},{9,11},{10,... | collective-permute-start | bytes 98312 | tf_op jit(solution)/shard_map/ppermute | solution.py:57
  61.3 3.1 %collective-permute-start.13 = (f32[16,512]{1,0:T(8,128)S(1)}, f32[16,512]{1,0:T(8,128)S(1)}, u32[]{:S(2)}, u32[]{:S(2)}) collective-permute-start(f32[16,512]{1,0:T(8,128)S(1)} %get-tuple-element.52), channel_id=1, source_target_pairs={{0,3},{1,0},{2,1},{3,2},{4,7},{5,4},{6,5},{7,6},{8,11},{9,8},{10,9... | collective-permute-start | bytes 98312 | tf_op jit(solution)/shard_map/ppermute | solution.py:57
  62.9 4.8 %collective-permute-start.12 = (f32[16,512]{1,0:T(8,128)S(1)}, f32[16,512]{1,0:T(8,128)S(1)}, u32[]{:S(2)}, u32[]{:S(2)}) collective-permute-start(f32[16,512]{1,0:T(8,128)S(1)} %get-tuple-element.53), channel_id=1, source_target_pairs={{0,1},{1,2},{2,3},{3,0},{4,5},{5,6},{6,7},{7,4},{8,9},{9,10},{10,1... | collective-permute-start | bytes 98312 | tf_op jit(solution)/shard_map/ppermute | solution.py:57
  78.8 1.9 %collective-permute-start.14 = (f32[224,512]{1,0:T(8,128)S(1)}, f32[224,512]{1,0:T(8,128)S(1)}, u32[]{:S(2)}, u32[]{:S(2)}) collective-permute-start(f32[224,512]{1,0:T(8,128)S(1)} %add_add_fusion.refs_0_), channel_id=1, source_target_pairs={{0,16},{16,0},{32,48},{48,32},{64,80},{80,64},{96,112},{112,96},{1... | collective-permute-start | bytes 1376264 | tf_op jit(solution)/shard_map/ppermute | solution.py:384
  79.3 2.1 %collective-permute-start.15 = (f32[224,512]{1,0:T(8,128)S(1)}, f32[224,512]{1,0:T(8,128)S(1)}, u32[]{:S(2)}, u32[]{:S(2)}) collective-permute-start(f32[224,512]{1,0:T(8,128)S(1)} %collective-permute-done.4.refs_1_), channel_id=1, source_target_pairs={{0,16},{16,0},{32,48},{48,32},{64,80},{80,64},{96,112},{112,96},{1... | collective-permute-start | bytes 1376264 | tf_op jit(solution)/shard_map/ppermute | solution.py:384
  79.3 2.7 %collective-permute-start.16 = (f32[224,512]{1,0:T(8,128)S(1)}, f32[224,512]{1,0:T(8,128)S(1)}, u32[]{:S(2)}, u32[]{:S(2)}) collective-permute-start(f32[224,512]{1,0:T(8,128)S(1)} %collective-permute-done.5.refs_2_), channel_id=1, source_target_pairs={{0,16},{16,0},{32,48},{48,32},{64,80},{80,64},{96,112},{112,96},{1... | collective-permute-start | bytes 1376264 | tf_op jit(solution)/shard_map/ppermute | solution.py:384
  79.8 2.9 %collective-permute-start.17 = (f32[224,512]{1,0:T(8,128)S(1)}, f32[224,512]{1,0:T(8,128)S(1)}, u32[]{:S(2)}, u32[]{:S(2)}) collective-permute-start(f32[224,512]{1,0:T(8,128)S(1)} %collective-permute-done.6.refs_3_), channel_id=1, source_target_pairs={{0,16},{16,0},{32,48},{48,32},{64,80},{80,64},{96,112},{112,96},{1... | collective-permute-start | bytes 1376264 | tf_op jit(solution)/shard_map/ppermute | solution.py:384
  79.9 12.8 %collective-permute-start.20 = (f32[16,512]{1,0:T(8,128)S(1)}, f32[16,512]{1,0:T(8,128)S(1)}, u32[]{:S(2)}, u32[]{:S(2)}) collective-permute-start(f32[16,512]{1,0:T(8,128)S(1)} %add_add_fusion.3), channel_id=1, source_target_pairs={{0,96},{16,112},{32,0},{48,16},{64,32},{80,48},{96,64},{112,80},{1... | collective-permute-start | bytes 98312 | tf_op jit(solution)/shard_map/ppermute | solution.py:83
  80.7 12.0 %collective-permute-start.19 = (f32[16,512]{1,0:T(8,128)S(1)}, f32[16,512]{1,0:T(8,128)S(1)}, u32[]{:S(2)}, u32[]{:S(2)}) collective-permute-start(f32[16,512]{1,0:T(8,128)S(1)} %add_add_fusion.3), channel_id=1, source_target_pairs={{0,64},{16,80},{32,96},{48,112},{64,0},{80,16},{96,32},{112,48},{1... | collective-permute-start | bytes 98312 | tf_op jit(solution)/shard_map/ppermute | solution.py:83
  81.4 11.3 %collective-permute-start.18 = (f32[16,512]{1,0:T(8,128)S(1)}, f32[16,512]{1,0:T(8,128)S(1)}, u32[]{:S(2)}, u32[]{:S(2)}) collective-permute-start(f32[16,512]{1,0:T(8,128)S(1)} %add_add_fusion.3), channel_id=1, source_target_pairs={{0,32},{16,48},{32,64},{48,80},{64,96},{80,112},{96,0},{112,16},{1... | collective-permute-start | bytes 98312 | tf_op jit(solution)/shard_map/ppermute | solution.py:83
  135.9 34.5 %all-to-all-start.1 = ((f32[16,64,512]{2,1,0:T(8,128)}), f32[16,64,512]{2,1,0:T(8,128)S(1)}, u32[]{:S(2)}, u32[]{:S(2)}) async-start(f32[16,64,512]{2,1,0:T(8,128)} %broadcast_in_dim.8), calls=%async_computation.1 | async-start | bytes 4194304 | tf_op jit(solution)/shard_map/all_to_all | solution.py:361
  140.7 3.9 %collective-permute-start.21 = (f32[256,512]{1,0:T(8,128)S(1)}, f32[256,512]{1,0:T(8,128)S(1)}, u32[]{:S(2)}, u32[]{:S(2)}) collective-permute-start(f32[256,512]{1,0:T(8,128)S(1)} %bitcast.12), channel_id=1, source_target_pairs={{0,16},{16,0},{32,48},{48,32},{64,80},{80,64},{96,112},{112,96},{1... | collective-permute-start | bytes 1572872 | tf_op jit(solution)/shard_map/ppermute | solution.py:79
  143.2 19.9 %copy-start.5 = (f32[8,224,512]{2,1,0:T(8,128)S(1)}, f32[8,224,512]{2,1,0:T(8,128)}, u32[]{:S(2)}) copy-start(f32[8,224,512]{2,1,0:T(8,128)} %get-tuple-element.28) | copy-start | bytes 11010052
  167.9 1.2 copy-start.2
  169.1 1.3 copy-start.6
  170.4 7.7 %copy-start.1 = (bf16[1024,1792]{1,0:T(8,128)(2,1)S(1)}, bf16[1024,1792]{1,0:T(8,128)(2,1)}, u32[]{:S(2)}) copy-start(bf16[1024,1792]{1,0:T(8,128)(2,1)} %gradient_ref.7) | copy-start | bytes 11010052
  170.4 7.7 %copy-start.3 = (bf16[512,1792]{1,0:T(8,128)(2,1)S(1)}, bf16[512,1792]{1,0:T(8,128)(2,1)}, u32[]{:S(2)}) copy-start(bf16[512,1792]{1,0:T(8,128)(2,1)} %copy-done.2) | copy-start | bytes 5505028
  173.0 1.3 collective-permute-start.22
  174.3 11.2 %collective-permute-start.25 = (f32[1,512]{1,0:T(1,128)S(1)}, f32[1,512]{1,0:T(1,128)S(1)}, u32[]{:S(2)}, u32[]{:S(2)}) collective-permute-start(f32[1,512]{1,0:T(1,128)S(1)} %add.209), channel_id=1, source_target_pairs={{0,96},{16,112},{32,0},{48,16},{64,32},{80,48},{96,64},{112,80},{1... | collective-permute-start | bytes 6152 | tf_op jit(solution)/shard_map/ppermute | solution.py:52
  175.8 9.8 %collective-permute-start.24 = (f32[1,512]{1,0:T(1,128)S(1)}, f32[1,512]{1,0:T(1,128)S(1)}, u32[]{:S(2)}, u32[]{:S(2)}) collective-permute-start(f32[1,512]{1,0:T(1,128)S(1)} %add.209), channel_id=1, source_target_pairs={{0,32},{16,48},{32,64},{48,80},{64,96},{80,112},{96,0},{112,16},{1... | collective-permute-start | bytes 6152 | tf_op jit(solution)/shard_map/ppermute | solution.py:52
  175.8 9.8 %collective-permute-start.23 = (f32[1,512]{1,0:T(1,128)S(1)}, f32[1,512]{1,0:T(1,128)S(1)}, u32[]{:S(2)}, u32[]{:S(2)}) collective-permute-start(f32[1,512]{1,0:T(1,128)S(1)} %add.209), channel_id=1, source_target_pairs={{0,64},{16,80},{32,96},{48,112},{64,0},{80,16},{96,32},{112,48},{1... | collective-permute-start | bytes 6152 | tf_op jit(solution)/shard_map/ppermute | solution.py:52
  178.0 3.1 %copy-start = (f32[1024,1792]{1,0:T(8,128)S(1)}, f32[1024,1792]{1,0:T(8,128)}, u32[]{:S(2)}) copy-start(f32[1024,1792]{1,0:T(8,128)} %momentum_ref.7) | copy-start | bytes 22020100
  181.1 4.5 %copy-start.4 = (bf16[1024,1792]{1,0:T(8,128)(2,1)S(1)}, bf16[1024,1792]{1,0:T(8,128)(2,1)}, u32[]{:S(2)}) copy-start(bf16[1024,1792]{1,0:T(8,128)(2,1)} %weight_ref.1) | copy-start | bytes 11010052
  181.1 4.9 %copy-start.7 = (bf16[512,1792]{1,0:T(8,128)(2,1)S(1)}, bf16[512,1792]{1,0:T(8,128)(2,1)}, u32[]{:S(2)}) copy-start(bf16[512,1792]{1,0:T(8,128)(2,1)} %copy-done.6) | copy-start | bytes 5505028
where the time goes:
time: 194 us; the launch traced here: 193 us
  Pallas kernels  61.3 us (32%)
  waiting for transfers between devices  42.5 us (22%)
  blocking collectives  39.5 us (20%)
  starting transfers between devices  32 us (16%)
  local copies, waits for them, and re-layouts  10.1 us (5%)
  other arithmetic  5.94 us (3%)
    all_to_all x1, blocking collectives, exchange(): return lax.all_to_all(array, 'col', 0, 0)  39.5 us
    ppermute x9, waiting for transfers between devices, ring_scatter(): lax.ppermute(pick(array, (place + s) % 4, size), axis, moves(s))  26.2 us
    pallas_call x1, Pallas kernels, inverse_of_factor(): pl.pallas_call(inverse_kernel, out_shape=square, scratch_shapes=[pltpu.VM...  18.4 us
    ppermute x9, starting transfers between devices, ring_scatter(): lax.ppermute(pick(array, (place + s) % 4, size), axis, moves(s))  13.8 us
    pallas_call x2, Pallas kernels, left_half(): pl.pallas_call(left_kernel, grid_spec=pltpu.PrefetchScalarGridSpec(num_sc...  13.7 us
    ppermute x6, waiting for transfers between devices, ring_parts(): return [array] + [lax.ppermute(array, 'row', moves(s)) for s in (1, 2, 3)]  11 us
    pallas_call x1, Pallas kernels, blended_times_left(): call(product_kernel, (rows // tile,), [pl.BlockSpec(memory_space=pltpu.SM...  9.98 us
    pallas_call x1, Pallas kernels, next_weight(): call(weight_kernel, (rows // tile,), [tall(tile, RANK), whole(1, RANK), w...  7.37 us
  transfers between devices with their start and end apart: 27, of which 13 were waited for; matrix products, arithmetic and copies ran while one was open for 1% of the time, Pallas kernels for 23%

commit v1 on v0

--- a/solution.py
+++ b/solution.py
@@ -223,7 +223,7 @@
 
 
 def product_kernel(place_ref, momentum_ref, gradient_ref, *refs):
-    parts, (product_ref, left_ref, high_ref, low_ref) = refs[:8], refs[8:]
+    parts, (product_ref, left_ref, whole_ref, high_ref, low_ref) = refs[:8], refs[8:]
 
     @pl.when(pl.program_id(0) == 0)
     def _():
@@ -231,10 +231,12 @@
         for i, part in enumerate(parts):
             at = 4 * (core if i < 4 else 1 - core) + (x + 4 - i % 4) % 4
             value = part[...]
-            left_ref[at] = value
+            whole_ref[at] = value
             high_ref[at], low_ref[at] = split(value)
 
-    count = left_ref.shape[0] * left_ref.shape[1]
+    step, chunks = pl.program_id(0), left_ref.shape[0]
+    left_ref[...] = whole_ref[pl.ds(step * chunks, chunks)]
+    count = whole_ref.shape[0] * whole_ref.shape[1]
     left = [ref[...].reshape(count, RANK) for ref in (high_ref, low_ref)]
     blended = split(momentum_ref[...] + gradient_ref[...].astype(jnp.float32))
     product_ref[...] = dot_split(blended, left, (1, 0))
@@ -248,9 +250,9 @@
         product_kernel,
         (rows // tile,),
         [pl.BlockSpec(memory_space=pltpu.SMEM), tall(tile, columns), tall(tile, columns)] + [whole(size, RANK)] * 8,
-        [tall(tile, RANK), whole(*shape)],
+        [tall(tile, RANK), pl.BlockSpec((8 * tile // rows, size, RANK), lambda i: (i, 0, 0))],
         [jax.ShapeDtypeStruct((rows, RANK), jnp.float32), jax.ShapeDtypeStruct(shape, jnp.float32)],
-        [pltpu.VMEM(shape, jnp.bfloat16)] * 2,
+        [pltpu.VMEM(shape, jnp.float32)] + [pltpu.VMEM(shape, jnp.bfloat16)] * 2,
         6 * rows * columns * RANK,
         6 * rows * columns + 8 * columns * RANK,
         "blended_times_left",
@@ -375,7 +377,9 @@
     given = left_half(jnp.reshape(1 - core, (1,)).astype(jnp.int32), momentum, gradient, basis_prev)
     taken = lax.ppermute(given, "row", other_core)
     kept = left_half(jnp.reshape(core, (1,)).astype(jnp.int32), momentum, gradient, basis_prev)
-    left_rows = ring_scatter(kept + taken, "row", x, along_x)
+    size = kept.shape[0] // 4
+    sums = [pick(kept, (x + s) % 4, size) + pick(taken, (x + s) % 4, size) for s in range(4)]
+    left_rows = total(sums[0], [lax.ppermute(sums[s], "row", along_x(s)) for s in (1, 2, 3)])
 
     parts = ring_parts(left_rows, along_x)
     gram_rows = core_scatter(dot(left_rows, left_rows, (0, 0), highest), core)

time: 194 us -> 193 us (level)
    ppermute x9 -> x6, waiting for transfers between devices: 26.2 us -> 6.48 us  [ring_scatter(): lax.ppermute(pick(array, (place + s) % 4, size), axis, moves(s))]
    ppermute x0 -> x3, waiting for transfers between devices: none -> 19.6 us  [on_device(): lax.ppermute(sums[s], 'row', along_x(s))]
    ppermute x0 -> x3, starting transfers between devices: none -> 4.38 us  [on_device(): lax.ppermute(sums[s], 'row', along_x(s))]
    ppermute x9 -> x6, starting transfers between devices: 13.8 us -> 9.51 us  [ring_scatter(): lax.ppermute(pick(array, (place + s) % 4, size), axis, moves(s))]
  transfers between devices with their start and end apart: 27 -> 27, of which waited for: 13 -> 14; matrix products, arithmetic and copies ran while one was open for 1% -> 1% of each run, Pallas kernels for 23% -> 23%
where the time goes in v1:
time: 193 us; the launch traced here: 192 us
  Pallas kernels  61.6 us (32%)
  waiting for transfers between devices  42.5 us (22%)
  blocking collectives  39.5 us (20%)
  starting transfers between devices  31.8 us (16%)
  local copies, waits for them, and re-layouts  9.08 us (5%)
  other arithmetic  5.54 us (3%)
    all_to_all x1, blocking collectives, exchange(): return lax.all_to_all(array, 'col', 0, 0)  39.5 us
    ppermute x3, waiting for transfers between devices, on_device(): lax.ppermute(sums[s], 'row', along_x(s))  19.6 us
    pallas_call x1, Pallas kernels, inverse_of_factor(): pl.pallas_call(inverse_kernel, out_shape=square, scratch_shapes=[pltpu.VM...  18.4 us
    pallas_call x2, Pallas kernels, left_half(): pl.pallas_call(left_kernel, grid_spec=pltpu.PrefetchScalarGridSpec(num_sc...  13.7 us
    ppermute x6, waiting for transfers between devices, ring_parts(): return [array] + [lax.ppermute(array, 'row', moves(s)) for s in (1, 2, 3)]  11 us
    pallas_call x1, Pallas kernels, blended_times_left(): call(product_kernel, (rows // tile,), [pl.BlockSpec(memory_space=pltpu.SM...  10.3 us
    ppermute x6, starting transfers between devices, ring_scatter(): lax.ppermute(pick(array, (place + s) % 4, size), axis, moves(s))  9.51 us
    pallas_call x1, Pallas kernels, next_weight(): call(weight_kernel, (rows // tile,), [tall(tile, RANK), whole(1, RANK), w...  7.37 us
  transfers between devices with their start and end apart: 27, of which 14 were waited for; matrix products, arithmetic and copies ran while one was open for 1% of the time, Pallas kernels for 23%

profile of v1, /device:TPU:1, one launch (start us, length us, event | category | flops | bytes accessed | tf_op | source)
XLA Modules:
  0.0 192.1 jit_solution(3508082201248754930)
XLA Ops:
  0.6 6.9 %left_half.3 = f32[896,512]{1,0:T(8,128)} custom-call(s32[1]{0:T(128)} %bitcast.2.half_ref, f32[1024,1792]{1,0:T(8,128)} %momentum_ref.7, bf16[1024,1792]{1,0:T(8,128)(2,1)} %gradient_ref.7, f32[1024,512]{1,0:T(8,128)} %basis_ref.3), custom_call_target="tpu_custom_call" | custom-call | flops 2818572288 | bytes 9175040 | tf_op jit(solution)/shard_map/left_half/pallas_call | solution.py:208
  7.5 1.4 collective-permute-start
  8.9 6.9 %left_half.2 = f32[896,512]{1,0:T(8,128)} custom-call(s32[1]{0:T(128)} %bitcast.1.half_ref, f32[1024,1792]{1,0:T(8,128)} %momentum_ref.7, bf16[1024,1792]{1,0:T(8,128)(2,1)} %gradient_ref.7, f32[1024,512]{1,0:T(8,128)} %basis_ref.3), custom_call_target="tpu_custom_call" | custom-call | flops 2818572288 | bytes 9175040 | tf_op jit(solution)/shard_map/left_half/pallas_call | solution.py:208
  15.8 1.6 dynamic-slice_add_fusion.3
  17.4 2.9 %collective-permute-start.1 = (f32[224,512]{1,0:T(8,128)S(1)}, f32[224,512]{1,0:T(8,128)}, u32[]{:S(2)}, u32[]{:S(2)}) collective-permute-start(f32[224,512]{1,0:T(8,128)S(1)} %get-tuple-element.45), channel_id=1, source_target_pairs={{0,64},{16,80},{32,96},{48,112},{64,0},{80,16},{96,32},{112,48},{1... | collective-permute-start | bytes 1376264 | tf_op jit(solution)/shard_map/ppermute | solution.py:382
  20.3 0.8 collective-permute-start.3
  21.2 0.6 collective-permute-start.2
  21.8 9.5 %collective-permute-done.1 = f32[224,512]{1,0:T(8,128)} collective-permute-done((f32[224,512]{1,0:T(8,128)S(1)}, f32[224,512]{1,0:T(8,128)}, u32[]{:S(2)}, u32[]{:S(2)}) %collective-permute-start.1) | collective-permute-done | bytes 458784 | tf_op jit(solution)/shard_map/ppermute | solution.py:382
  31.3 10.0 %collective-permute-done.3 = f32[224,512]{1,0:T(8,128)} collective-permute-done((f32[224,512]{1,0:T(8,128)S(1)}, f32[224,512]{1,0:T(8,128)}, u32[]{:S(2)}, u32[]{:S(2)}) %collective-permute-start.3) | collective-permute-done | bytes 458784 | tf_op jit(solution)/shard_map/ppermute | solution.py:382
  41.3 0.0 collective-permute-done.2
  41.4 1.7 add_add_fusion.refs_0_
  43.0 1.1 fusion
  44.2 0.8 collective-permute-start.7
  45.0 1.5 collective-permute-done.7
  46.6 0.1 dynamic-slice_add_fusion
  46.7 3.0 %collective-permute-start.8 = (f32[64,512]{1,0:T(8,128)S(1)}, f32[64,512]{1,0:T(8,128)S(1)}, u32[]{:S(2)}, u32[]{:S(2)}) collective-permute-start(f32[64,512]{1,0:T(8,128)S(1)} %get-tuple-element.48), channel_id=1, source_target_pairs={{0,8},{1,9},{2,10},{3,11},{4,12},{5,13},{6,14},{7,15},{8,0},{9,1},... | collective-permute-start | bytes 393224 | tf_op jit(solution)/shard_map/ppermute | solution.py:57
  49.7 0.8 collective-permute-start.10
  50.5 0.7 collective-permute-start.9
  51.2 2.3 %collective-permute-start.6 = (f32[224,512]{1,0:T(8,128)S(1)}, f32[224,512]{1,0:T(8,128)S(1)}, u32[]{:S(2)}, u32[]{:S(2)}) collective-permute-start(f32[224,512]{1,0:T(8,128)S(1)} %add_add_fusion.refs_0_), channel_id=1, source_target_pairs={{0,96},{16,112},{32,0},{48,16},{64,32},{80,48},{96,64},{112,80},{1... | collective-permute-start | bytes 1376264 | tf_op jit(solution)/shard_map/ppermute | solution.py:83
  53.5 0.6 collective-permute-start.5
  54.1 0.5 collective-permute-start.4
  54.6 1.5 collective-permute-done.10
  56.2 3.7 %collective-permute-start.11 = (f32[16,512]{1,0:T(8,128)S(1)}, f32[16,512]{1,0:T(8,128)S(1)}, u32[]{:S(2)}, u32[]{:S(2)}) collective-permute-start(f32[16,512]{1,0:T(8,128)S(1)} %get-tuple-element.51), channel_id=1, source_target_pairs={{0,2},{1,3},{2,0},{3,1},{4,6},{5,7},{6,4},{7,5},{8,10},{9,11},{10,... | collective-permute-start | bytes 98312 | tf_op jit(solution)/shard_map/ppermute | solution.py:57
  59.9 0.4 collective-permute-start.13
  60.3 1.2 collective-permute-done.11
  61.5 1.0 collective-permute-start.12
  62.5 0.5 collective-permute-done.13
  62.9 3.3 %collective-permute-done.12 = f32[16,512]{1,0:T(8,128)S(1)} collective-permute-done((f32[16,512]{1,0:T(8,128)S(1)}, f32[16,512]{1,0:T(8,128)S(1)}, u32[]{:S(2)}, u32[]{:S(2)}) %collective-permute-start.12) | collective-permute-done | bytes 32800 | tf_op jit(solution)/shard_map/ppermute | solution.py:57
  66.3 11.0 %collective-permute-done.4.refs_1_ = f32[224,512]{1,0:T(8,128)S(1)} collective-permute-done((f32[224,512]{1,0:T(8,128)S(1)}, f32[224,512]{1,0:T(8,128)S(1)}, u32[]{:S(2)}, u32[]{:S(2)}) %collective-permute-start.4) | collective-permute-done | bytes 458784 | tf_op jit(solution)/shard_map/ppermute | solution.py:83
  77.3 0.5 collective-permute-start.14
  77.8 0.5 collective-permute-start.16
  78.3 0.1 pad_add_fusion.place_ref
  78.4 0.3 collective-permute-start.20
  78.7 0.5 collective-permute-done.14.refs_4_
  79.2 0.6 collective-permute-start.19
  79.8 0.1 collective-permute-done.15.refs_5_
  79.9 0.3 collective-permute-start.18
  80.1 0.4 collective-permute-done.16.refs_6_
  80.5 0.7 collective-permute-done.17.refs_7_
  81.2 10.3 %blended_times_left.1 = (f32[1024,512]{1,0:T(8,128)S(1)}, f32[8,224,512]{2,1,0:T(8,128)}) custom-call(s32[2]{0:T(128)S(1)} %pad_add_fusion.place_ref, f32[1024,1792]{1,0:T(8,128)} %momentum_ref.7, bf16[1024,1792]{1,0:T(8,128)(2,1)} %gradient_ref.7, f32[224,512]{1,0:T(8,128)S(1)} %add_add_fusion.refs_0_, f32[224,512]{1,0:T(8,128)S(1)} %collective-permute-done.4.refs_1_, ...), custom_call_target="tpu_custom_call" | custom-call | flops 5637144576 | bytes 18350080 | tf_op jit(solution)/shard_map/blended_times_left/pallas_call | solution.py:249
  91.5 0.1 broadcast_in_dim.7
  91.6 0.3 pad_maximum_fusion
  91.9 39.5 %all_to_all.10 = f32[16,80,512]{2,1,0:T(8,128)} all-to-all(f32[16,80,512]{2,1,0:T(8,128)S(1)} %pad_maximum_fusion), channel_id=1, replica_groups=mesh['row'=8,'col'=16] {'col'}, dimensions={0} | all-to-all | bytes 5242880 | tf_op jit(solution)/shard_map/all_to_all | solution.py:363
  131.4 1.8 slice_reduce_fusion
  133.2 1.6 broadcast_in_dim.8
  134.8 3.7 %all-to-all-start.1 = ((f32[16,64,512]{2,1,0:T(8,128)}), f32[16,64,512]{2,1,0:T(8,128)S(1)}, u32[]{:S(2)}, u32[]{:S(2)}) async-start(f32[16,64,512]{2,1,0:T(8,128)} %broadcast_in_dim.8), calls=%async_computation.1 | async-start | bytes 4194304 | tf_op jit(solution)/shard_map/all_to_all | solution.py:363
  138.5 1.1 slice.8
  139.6 2.1 %collective-permute-start.21 = (f32[256,512]{1,0:T(8,128)S(1)}, f32[256,512]{1,0:T(8,128)S(1)}, u32[]{:S(2)}, u32[]{:S(2)}) collective-permute-start(f32[256,512]{1,0:T(8,128)S(1)} %bitcast.12), channel_id=1, source_target_pairs={{0,16},{16,0},{32,48},{48,32},{64,80},{80,64},{96,112},{112,96},{1... | collective-permute-start | bytes 1572872 | tf_op jit(solution)/shard_map/ppermute | solution.py:79
  141.8 0.1 broadcast_in_dim.6
  141.9 1.4 collective-permute-done.21
  143.3 18.4 %inverse_of_factor.1.inverse_ref = f32[512,512]{1,0:T(8,128)S(1)} custom-call(f32[512,512]{1,0:T(8,128)S(1)} %constant_dynamic-update-slice_fusion.gram_ref), custom_call_target="tpu_custom_call" | custom-call | flops 268435456 | bytes 2097152 | tf_op jit(solution)/shard_map/inverse_of_factor/pallas_call | solution.py:134
  161.7 4.7 %ortho_halves.1 = (bf16[512,1792]{1,0:T(8,128)(2,1)S(1)}, bf16[512,1792]{1,0:T(8,128)(2,1)S(1)}) custom-call(f32[1792,512]{1,0:T(8,128)S(1)} %bitcast.11, f32[512,512]{1,0:T(8,128)S(1)} %inverse_of_factor.1.inverse_ref), custom_call_target="tpu_custom_call" | custom-call | flops 2818572288 | bytes 7340032 | tf_op jit(solution)/shard_map/ortho_halves/pallas_call | solution.py:274
  166.5 1.2 copy-done.2
  167.7 1.3 copy-done.6
  169.0 2.6 %right_and_squares.1 = (f32[1024,512]{1,0:T(8,128)S(1)}, f32[1,512]{1,0:T(1,128)S(1)}) custom-call(f32[1024,512]{1,0:T(8,128)S(1)} %bitcast.9, f32[512,512]{1,0:T(8,128)S(1)} %inverse_of_factor.1.inverse_ref), custom_call_target="tpu_custom_call" | custom-call | flops 1610612736 | bytes 4194304 | tf_op jit(solution)/shard_map/right_and_squares/pallas_call | solution.py:301
  171.6 0.5 collective-permute-start.22
  172.1 0.8 collective-permute-done.22
  172.9 1.4 collective-permute-start.25
  174.3 0.1 collective-permute-start.24
  174.4 2.3 %collective-permute-start.23 = (f32[1,512]{1,0:T(1,128)S(1)}, f32[1,512]{1,0:T(1,128)S(1)}, u32[]{:S(2)}, u32[]{:S(2)}) collective-permute-start(f32[1,512]{1,0:T(1,128)S(1)} %add.236), channel_id=1, source_target_pairs={{0,64},{16,80},{32,96},{48,112},{64,0},{80,16},{96,32},{112,48},{1... | collective-permute-start | bytes 6152 | tf_op jit(solution)/shard_map/ppermute | solution.py:52
  176.6 3.1 %copy-done = f32[1024,1792]{1,0:T(8,128)S(1)} copy-done((f32[1024,1792]{1,0:T(8,128)S(1)}, f32[1024,1792]{1,0:T(8,128)}, u32[]{:S(2)}) %copy-start) | copy-done | bytes 7340056
  179.7 4.4 %next_momentum.1 = f32[1024,1792]{1,0:T(8,128)} custom-call(f32[1024,512]{1,0:T(8,128)S(1)} %get-tuple-element.39.right_ref, bf16[512,1792]{1,0:T(8,128)(2,1)S(1)} %copy-done.3, f32[1024,1792]{1,0:T(8,128)S(1)} %copy-done, bf16[1024,1792]{1,0:T(8,128)(2,1)S(1)} %copy-done.1), custom_call_target="tpu_custom_call" | custom-call | flops 1879048192 | bytes 18350080 | tf_op jit(solution)/shard_map/next_momentum/pallas_call | solution.py:323
  184.2 0.5 copy-done.7
  184.7 7.4 %next_weight.1 = (f32[1024,512]{1,0:T(8,128)}, bf16[1024,1792]{1,0:T(8,128)(2,1)}) custom-call(f32[1024,512]{1,0:T(8,128)S(1)} %get-tuple-element.39.right_ref, f32[1,512]{1,0:T(1,128)S(1)} %add_add_fusion.4.squares_ref, bf16[512,1792]{1,0:T(8,128)(2,1)S(1)} %copy-done.3, bf16[512,1792]{1,0:T(8,128)(2,1)S(1)} %copy-done.7, bf16[1024,1792]{1,0:T(8,128)(2,1)S(1)} %copy-done.4), custom_call_target="tpu_custom_call" | custom-call | flops 5637144576 | bytes 11534336 | tf_op jit(solution)/shard_map/next_weight/pallas_call | solution.py:348
  (36 shorter events, 0.3 us)
Async XLA Ops:
  7.5 8.3 %collective-permute-start = (f32[896,512]{1,0:T(8,128)}, f32[896,512]{1,0:T(8,128)S(1)}, u32[]{:S(2)}, u32[]{:S(2)}) collective-permute-start(f32[896,512]{1,0:T(8,128)} %left_half.3), channel_id=1, source_target_pairs={{0,16},{16,0},{32,48},{48,32},{64,80},{80,64},{96,112},{112,96},{1... | collective-permute-start | bytes 5505032 | tf_op jit(solution)/shard_map/ppermute | solution.py:378
  17.4 13.9 %collective-permute-start.1 = (f32[224,512]{1,0:T(8,128)S(1)}, f32[224,512]{1,0:T(8,128)}, u32[]{:S(2)}, u32[]{:S(2)}) collective-permute-start(f32[224,512]{1,0:T(8,128)S(1)} %get-tuple-element.45), channel_id=1, source_target_pairs={{0,64},{16,80},{32,96},{48,112},{64,0},{80,16},{96,32},{112,48},{1... | collective-permute-start | bytes 1376264 | tf_op jit(solution)/shard_map/ppermute | solution.py:382
  20.3 21.0 %collective-permute-start.3 = (f32[224,512]{1,0:T(8,128)S(1)}, f32[224,512]{1,0:T(8,128)}, u32[]{:S(2)}, u32[]{:S(2)}) collective-permute-start(f32[224,512]{1,0:T(8,128)S(1)} %get-tuple-element.46), channel_id=1, source_target_pairs={{0,96},{16,112},{32,0},{48,16},{64,32},{80,48},{96,64},{112,80},{1... | collective-permute-start | bytes 1376264 | tf_op jit(solution)/shard_map/ppermute | solution.py:382
  21.2 20.2 %collective-permute-start.2 = (f32[224,512]{1,0:T(8,128)S(1)}, f32[224,512]{1,0:T(8,128)}, u32[]{:S(2)}, u32[]{:S(2)}) collective-permute-start(f32[224,512]{1,0:T(8,128)S(1)} %get-tuple-element.47), channel_id=1, source_target_pairs={{0,32},{16,48},{32,64},{48,80},{64,96},{80,112},{96,0},{112,16},{1... | collective-permute-start | bytes 1376264 | tf_op jit(solution)/shard_map/ppermute | solution.py:382
  44.2 2.4 %collective-permute-start.7 = (f32[256,512]{1,0:T(8,128)S(1)}, f32[256,512]{1,0:T(8,128)S(1)}, u32[]{:S(2)}, u32[]{:S(2)}) collective-permute-start(f32[256,512]{1,0:T(8,128)S(1)} %constant_dynamic-slice_fusion.6), channel_id=1, source_target_pairs={{0,16},{16,0},{32,48},{48,32},{64,80},{80,64},{96,112},{112,96},{1... | collective-permute-start | bytes 1572872 | tf_op jit(solution)/shard_map/ppermute | solution.py:72
  46.7 7.4 %collective-permute-start.8 = (f32[64,512]{1,0:T(8,128)S(1)}, f32[64,512]{1,0:T(8,128)S(1)}, u32[]{:S(2)}, u32[]{:S(2)}) collective-permute-start(f32[64,512]{1,0:T(8,128)S(1)} %get-tuple-element.48), channel_id=1, source_target_pairs={{0,8},{1,9},{2,10},{3,11},{4,12},{5,13},{6,14},{7,15},{8,0},{9,1},... | collective-permute-start | bytes 393224 | tf_op jit(solution)/shard_map/ppermute | solution.py:57
  49.7 6.5 %collective-permute-start.10 = (f32[64,512]{1,0:T(8,128)S(1)}, f32[64,512]{1,0:T(8,128)S(1)}, u32[]{:S(2)}, u32[]{:S(2)}) collective-permute-start(f32[64,512]{1,0:T(8,128)S(1)} %get-tuple-element.49), channel_id=1, source_target_pairs={{0,12},{1,13},{2,14},{3,15},{4,0},{5,1},{6,2},{7,3},{8,4},{9,5},{1... | collective-permute-start | bytes 393224 | tf_op jit(solution)/shard_map/ppermute | solution.py:57
  50.5 5.7 %collective-permute-start.9 = (f32[64,512]{1,0:T(8,128)S(1)}, f32[64,512]{1,0:T(8,128)S(1)}, u32[]{:S(2)}, u32[]{:S(2)}) collective-permute-start(f32[64,512]{1,0:T(8,128)S(1)} %get-tuple-element.50), channel_id=1, source_target_pairs={{0,4},{1,5},{2,6},{3,7},{4,8},{5,9},{6,10},{7,11},{8,12},{9,13},{1... | collective-permute-start | bytes 393224 | tf_op jit(solution)/shard_map/ppermute | solution.py:57
  51.2 15.1 %collective-permute-start.6 = (f32[224,512]{1,0:T(8,128)S(1)}, f32[224,512]{1,0:T(8,128)S(1)}, u32[]{:S(2)}, u32[]{:S(2)}) collective-permute-start(f32[224,512]{1,0:T(8,128)S(1)} %add_add_fusion.refs_0_), channel_id=1, source_target_pairs={{0,96},{16,112},{32,0},{48,16},{64,32},{80,48},{96,64},{112,80},{1... | collective-permute-start | bytes 1376264 | tf_op jit(solution)/shard_map/ppermute | solution.py:83
  53.5 12.7 %collective-permute-start.5 = (f32[224,512]{1,0:T(8,128)S(1)}, f32[224,512]{1,0:T(8,128)S(1)}, u32[]{:S(2)}, u32[]{:S(2)}) collective-permute-start(f32[224,512]{1,0:T(8,128)S(1)} %add_add_fusion.refs_0_), channel_id=1, source_target_pairs={{0,64},{16,80},{32,96},{48,112},{64,0},{80,16},{96,32},{112,48},{1... | collective-permute-start | bytes 1376264 | tf_op jit(solution)/shard_map/ppermute | solution.py:83
  54.1 23.2 %collective-permute-start.4 = (f32[224,512]{1,0:T(8,128)S(1)}, f32[224,512]{1,0:T(8,128)S(1)}, u32[]{:S(2)}, u32[]{:S(2)}) collective-permute-start(f32[224,512]{1,0:T(8,128)S(1)} %add_add_fusion.refs_0_), channel_id=1, source_target_pairs={{0,32},{16,48},{32,64},{48,80},{64,96},{80,112},{96,0},{112,16},{1... | collective-permute-start | bytes 1376264 | tf_op jit(solution)/shard_map/ppermute | solution.py:83
  56.2 5.3 %collective-permute-start.11 = (f32[16,512]{1,0:T(8,128)S(1)}, f32[16,512]{1,0:T(8,128)S(1)}, u32[]{:S(2)}, u32[]{:S(2)}) collective-permute-start(f32[16,512]{1,0:T(8,128)S(1)} %get-tuple-element.51), channel_id=1, source_target_pairs={{0,2},{1,3},{2,0},{3,1},{4,6},{5,7},{6,4},{7,5},{8,10},{9,11},{10,... | collective-permute-start | bytes 98312 | tf_op jit(solution)/shard_map/ppermute | solution.py:57
  59.9 3.1 %collective-permute-start.13 = (f32[16,512]{1,0:T(8,128)S(1)}, f32[16,512]{1,0:T(8,128)S(1)}, u32[]{:S(2)}, u32[]{:S(2)}) collective-permute-start(f32[16,512]{1,0:T(8,128)S(1)} %get-tuple-element.52), channel_id=1, source_target_pairs={{0,3},{1,0},{2,1},{3,2},{4,7},{5,4},{6,5},{7,6},{8,11},{9,8},{10,9... | collective-permute-start | bytes 98312 | tf_op jit(solution)/shard_map/ppermute | solution.py:57
  61.5 4.8 %collective-permute-start.12 = (f32[16,512]{1,0:T(8,128)S(1)}, f32[16,512]{1,0:T(8,128)S(1)}, u32[]{:S(2)}, u32[]{:S(2)}) collective-permute-start(f32[16,512]{1,0:T(8,128)S(1)} %get-tuple-element.53), channel_id=1, source_target_pairs={{0,1},{1,2},{2,3},{3,0},{4,5},{5,6},{6,7},{7,4},{8,9},{9,10},{10,1... | collective-permute-start | bytes 98312 | tf_op jit(solution)/shard_map/ppermute | solution.py:57
  77.3 1.9 %collective-permute-start.14 = (f32[224,512]{1,0:T(8,128)S(1)}, f32[224,512]{1,0:T(8,128)S(1)}, u32[]{:S(2)}, u32[]{:S(2)}) collective-permute-start(f32[224,512]{1,0:T(8,128)S(1)} %add_add_fusion.refs_0_), channel_id=1, source_target_pairs={{0,16},{16,0},{32,48},{48,32},{64,80},{80,64},{96,112},{112,96},{1... | collective-permute-start | bytes 1376264 | tf_op jit(solution)/shard_map/ppermute | solution.py:388
  77.8 2.1 %collective-permute-start.15 = (f32[224,512]{1,0:T(8,128)S(1)}, f32[224,512]{1,0:T(8,128)S(1)}, u32[]{:S(2)}, u32[]{:S(2)}) collective-permute-start(f32[224,512]{1,0:T(8,128)S(1)} %collective-permute-done.4.refs_1_), channel_id=1, source_target_pairs={{0,16},{16,0},{32,48},{48,32},{64,80},{80,64},{96,112},{112,96},{1... | collective-permute-start | bytes 1376264 | tf_op jit(solution)/shard_map/ppermute | solution.py:388
  77.8 2.7 %collective-permute-start.16 = (f32[224,512]{1,0:T(8,128)S(1)}, f32[224,512]{1,0:T(8,128)S(1)}, u32[]{:S(2)}, u32[]{:S(2)}) collective-permute-start(f32[224,512]{1,0:T(8,128)S(1)} %collective-permute-done.5.refs_2_), channel_id=1, source_target_pairs={{0,16},{16,0},{32,48},{48,32},{64,80},{80,64},{96,112},{112,96},{1... | collective-permute-start | bytes 1376264 | tf_op jit(solution)/shard_map/ppermute | solution.py:388
  78.3 2.9 %collective-permute-start.17 = (f32[224,512]{1,0:T(8,128)S(1)}, f32[224,512]{1,0:T(8,128)S(1)}, u32[]{:S(2)}, u32[]{:S(2)}) collective-permute-start(f32[224,512]{1,0:T(8,128)S(1)} %collective-permute-done.6.refs_3_), channel_id=1, source_target_pairs={{0,16},{16,0},{32,48},{48,32},{64,80},{80,64},{96,112},{112,96},{1... | collective-permute-start | bytes 1376264 | tf_op jit(solution)/shard_map/ppermute | solution.py:388
  78.4 13.1 %collective-permute-start.20 = (f32[16,512]{1,0:T(8,128)S(1)}, f32[16,512]{1,0:T(8,128)S(1)}, u32[]{:S(2)}, u32[]{:S(2)}) collective-permute-start(f32[16,512]{1,0:T(8,128)S(1)} %add_add_fusion.3), channel_id=1, source_target_pairs={{0,96},{16,112},{32,0},{48,16},{64,32},{80,48},{96,64},{112,80},{1... | collective-permute-start | bytes 98312 | tf_op jit(solution)/shard_map/ppermute | solution.py:83
  79.2 12.3 %collective-permute-start.19 = (f32[16,512]{1,0:T(8,128)S(1)}, f32[16,512]{1,0:T(8,128)S(1)}, u32[]{:S(2)}, u32[]{:S(2)}) collective-permute-start(f32[16,512]{1,0:T(8,128)S(1)} %add_add_fusion.3), channel_id=1, source_target_pairs={{0,64},{16,80},{32,96},{48,112},{64,0},{80,16},{96,32},{112,48},{1... | collective-permute-start | bytes 98312 | tf_op jit(solution)/shard_map/ppermute | solution.py:83
  79.9 11.6 %collective-permute-start.18 = (f32[16,512]{1,0:T(8,128)S(1)}, f32[16,512]{1,0:T(8,128)S(1)}, u32[]{:S(2)}, u32[]{:S(2)}) collective-permute-start(f32[16,512]{1,0:T(8,128)S(1)} %add_add_fusion.3), channel_id=1, source_target_pairs={{0,32},{16,48},{32,64},{48,80},{64,96},{80,112},{96,0},{112,16},{1... | collective-permute-start | bytes 98312 | tf_op jit(solution)/shard_map/ppermute | solution.py:83
  134.8 34.2 %all-to-all-start.1 = ((f32[16,64,512]{2,1,0:T(8,128)}), f32[16,64,512]{2,1,0:T(8,128)S(1)}, u32[]{:S(2)}, u32[]{:S(2)}) async-start(f32[16,64,512]{2,1,0:T(8,128)} %broadcast_in_dim.8), calls=%async_computation.1 | async-start | bytes 4194304 | tf_op jit(solution)/shard_map/all_to_all | solution.py:363
  139.6 3.7 %collective-permute-start.21 = (f32[256,512]{1,0:T(8,128)S(1)}, f32[256,512]{1,0:T(8,128)S(1)}, u32[]{:S(2)}, u32[]{:S(2)}) collective-permute-start(f32[256,512]{1,0:T(8,128)S(1)} %bitcast.12), channel_id=1, source_target_pairs={{0,16},{16,0},{32,48},{48,32},{64,80},{80,64},{96,112},{112,96},{1... | collective-permute-start | bytes 1572872 | tf_op jit(solution)/shard_map/ppermute | solution.py:79
  141.9 19.8 %copy-start.5 = (f32[8,224,512]{2,1,0:T(8,128)S(1)}, f32[8,224,512]{2,1,0:T(8,128)}, u32[]{:S(2)}) copy-start(f32[8,224,512]{2,1,0:T(8,128)} %get-tuple-element.28) | copy-start | bytes 11010052
  166.5 1.2 copy-start.2
  167.7 1.3 copy-start.6
  169.0 7.7 %copy-start.1 = (bf16[1024,1792]{1,0:T(8,128)(2,1)S(1)}, bf16[1024,1792]{1,0:T(8,128)(2,1)}, u32[]{:S(2)}) copy-start(bf16[1024,1792]{1,0:T(8,128)(2,1)} %gradient_ref.7) | copy-start | bytes 11010052
  169.0 7.7 %copy-start.3 = (bf16[512,1792]{1,0:T(8,128)(2,1)S(1)}, bf16[512,1792]{1,0:T(8,128)(2,1)}, u32[]{:S(2)}) copy-start(bf16[512,1792]{1,0:T(8,128)(2,1)} %copy-done.2) | copy-start | bytes 5505028
  171.6 1.3 collective-permute-start.22
  172.9 11.2 %collective-permute-start.25 = (f32[1,512]{1,0:T(1,128)S(1)}, f32[1,512]{1,0:T(1,128)S(1)}, u32[]{:S(2)}, u32[]{:S(2)}) collective-permute-start(f32[1,512]{1,0:T(1,128)S(1)} %add.236), channel_id=1, source_target_pairs={{0,96},{16,112},{32,0},{48,16},{64,32},{80,48},{96,64},{112,80},{1... | collective-permute-start | bytes 6152 | tf_op jit(solution)/shard_map/ppermute | solution.py:52
  174.3 9.9 %collective-permute-start.24 = (f32[1,512]{1,0:T(1,128)S(1)}, f32[1,512]{1,0:T(1,128)S(1)}, u32[]{:S(2)}, u32[]{:S(2)}) collective-permute-start(f32[1,512]{1,0:T(1,128)S(1)} %add.236), channel_id=1, source_target_pairs={{0,32},{16,48},{32,64},{48,80},{64,96},{80,112},{96,0},{112,16},{1... | collective-permute-start | bytes 6152 | tf_op jit(solution)/shard_map/ppermute | solution.py:52
  174.4 9.8 %collective-permute-start.23 = (f32[1,512]{1,0:T(1,128)S(1)}, f32[1,512]{1,0:T(1,128)S(1)}, u32[]{:S(2)}, u32[]{:S(2)}) collective-permute-start(f32[1,512]{1,0:T(1,128)S(1)} %add.236), channel_id=1, source_target_pairs={{0,64},{16,80},{32,96},{48,112},{64,0},{80,16},{96,32},{112,48},{1... | collective-permute-start | bytes 6152 | tf_op jit(solution)/shard_map/ppermute | solution.py:52
  176.6 3.1 %copy-start = (f32[1024,1792]{1,0:T(8,128)S(1)}, f32[1024,1792]{1,0:T(8,128)}, u32[]{:S(2)}) copy-start(f32[1024,1792]{1,0:T(8,128)} %momentum_ref.7) | copy-start | bytes 22020100
  179.7 4.5 %copy-start.4 = (bf16[1024,1792]{1,0:T(8,128)(2,1)S(1)}, bf16[1024,1792]{1,0:T(8,128)(2,1)}, u32[]{:S(2)}) copy-start(bf16[1024,1792]{1,0:T(8,128)(2,1)} %weight_ref.1) | copy-start | bytes 11010052
  179.7 4.9 %copy-start.7 = (bf16[512,1792]{1,0:T(8,128)(2,1)S(1)}, bf16[512,1792]{1,0:T(8,128)(2,1)}, u32[]{:S(2)}) copy-start(bf16[512,1792]{1,0:T(8,128)(2,1)} %copy-done.6) | copy-start | bytes 5505028

commit v2 on v1

--- a/solution.py
+++ b/solution.py
@@ -135,8 +135,8 @@
         inverse_kernel,
         out_shape=square,
         scratch_shapes=[pltpu.VMEM((RANK, RANK), jnp.float32)] * 2,
-        compiler_params=pltpu.CompilerParams(vmem_limit_bytes=32 * 2**20),
-        cost_estimate=pl.CostEstimate(flops=2 * RANK**3, bytes_accessed=8 * RANK**2, transcendentals=RANK),
+        compiler_params=pltpu.CompilerParams(vmem_limit_bytes=12 * 2**20),
+        cost_estimate=pl.CostEstimate(flops=24 * RANK**3, bytes_accessed=8 * RANK**2, transcendentals=RANK),
         name="inverse_of_factor",
     )(gram_sum)
 

time: 193 us -> 193 us (level)
  no operation moved by 1% of the time
where the time goes in v2:
time: 193 us; the launch traced here: 192 us
  Pallas kernels  61.6 us (32%)
  waiting for transfers between devices  42.5 us (22%)
  blocking collectives  39.5 us (20%)
  starting transfers between devices  31.8 us (16%)
  local copies, waits for them, and re-layouts  9.08 us (5%)
  other arithmetic  5.54 us (3%)
    all_to_all x1, blocking collectives, exchange(): return lax.all_to_all(array, 'col', 0, 0)  39.5 us
    ppermute x3, waiting for transfers between devices, on_device(): lax.ppermute(sums[s], 'row', along_x(s))  19.6 us
    pallas_call x1, Pallas kernels, inverse_of_factor(): pl.pallas_call(inverse_kernel, out_shape=square, scratch_shapes=[pltpu.VM...  18.4 us
    pallas_call x2, Pallas kernels, left_half(): pl.pallas_call(left_kernel, grid_spec=pltpu.PrefetchScalarGridSpec(num_sc...  13.7 us
    ppermute x6, waiting for transfers between devices, ring_parts(): return [array] + [lax.ppermute(array, 'row', moves(s)) for s in (1, 2, 3)]  11 us
    pallas_call x1, Pallas kernels, blended_times_left(): call(product_kernel, (rows // tile,), [pl.BlockSpec(memory_space=pltpu.SM...  10.3 us
    ppermute x6, starting transfers between devices, ring_scatter(): lax.ppermute(pick(array, (place + s) % 4, size), axis, moves(s))  9.51 us
    pallas_call x1, Pallas kernels, next_weight(): call(weight_kernel, (rows // tile,), [tall(tile, RANK), whole(1, RANK), w...  7.37 us
  transfers between devices with their start and end apart: 27, of which 14 were waited for; matrix products, arithmetic and copies ran while one was open for 1% of the time, Pallas kernels for 23%

profile of v2, /device:TPU:1, one launch (start us, length us, event | category | flops | bytes accessed | tf_op | source)
XLA Modules:
  0.0 192.1 jit_solution(4750593406081040551)
XLA Ops:
  0.6 6.9 %left_half.3 = f32[896,512]{1,0:T(8,128)} custom-call(s32[1]{0:T(128)} %bitcast.2.half_ref, f32[1024,1792]{1,0:T(8,128)} %momentum_ref.7, bf16[1024,1792]{1,0:T(8,128)(2,1)} %gradient_ref.7, f32[1024,512]{1,0:T(8,128)} %basis_ref.3), custom_call_target="tpu_custom_call" | custom-call | flops 2818572288 | bytes 9175040 | tf_op jit(solution)/shard_map/left_half/pallas_call | solution.py:208
  7.5 1.4 collective-permute-start
  8.9 6.9 %left_half.2 = f32[896,512]{1,0:T(8,128)} custom-call(s32[1]{0:T(128)} %bitcast.1.half_ref, f32[1024,1792]{1,0:T(8,128)} %momentum_ref.7, bf16[1024,1792]{1,0:T(8,128)(2,1)} %gradient_ref.7, f32[1024,512]{1,0:T(8,128)} %basis_ref.3), custom_call_target="tpu_custom_call" | custom-call | flops 2818572288 | bytes 9175040 | tf_op jit(solution)/shard_map/left_half/pallas_call | solution.py:208
  15.8 1.6 dynamic-slice_add_fusion.3
  17.4 2.9 %collective-permute-start.1 = (f32[224,512]{1,0:T(8,128)S(1)}, f32[224,512]{1,0:T(8,128)}, u32[]{:S(2)}, u32[]{:S(2)}) collective-permute-start(f32[224,512]{1,0:T(8,128)S(1)} %get-tuple-element.45), channel_id=1, source_target_pairs={{0,64},{16,80},{32,96},{48,112},{64,0},{80,16},{96,32},{112,48},{1... | collective-permute-start | bytes 1376264 | tf_op jit(solution)/shard_map/ppermute | solution.py:382
  20.3 0.8 collective-permute-start.3
  21.2 0.6 collective-permute-start.2
  21.8 9.5 %collective-permute-done.1 = f32[224,512]{1,0:T(8,128)} collective-permute-done((f32[224,512]{1,0:T(8,128)S(1)}, f32[224,512]{1,0:T(8,128)}, u32[]{:S(2)}, u32[]{:S(2)}) %collective-permute-start.1) | collective-permute-done | bytes 458784 | tf_op jit(solution)/shard_map/ppermute | solution.py:382
  31.3 10.0 %collective-permute-done.3 = f32[224,512]{1,0:T(8,128)} collective-permute-done((f32[224,512]{1,0:T(8,128)S(1)}, f32[224,512]{1,0:T(8,128)}, u32[]{:S(2)}, u32[]{:S(2)}) %collective-permute-start.3) | collective-permute-done | bytes 458784 | tf_op jit(solution)/shard_map/ppermute | solution.py:382
  41.3 0.0 collective-permute-done.2
  41.4 1.7 add_add_fusion.refs_0_
  43.0 1.1 fusion
  44.2 0.8 collective-permute-start.7
  45.0 1.5 collective-permute-done.7
  46.6 0.1 dynamic-slice_add_fusion
  46.7 3.0 %collective-permute-start.8 = (f32[64,512]{1,0:T(8,128)S(1)}, f32[64,512]{1,0:T(8,128)S(1)}, u32[]{:S(2)}, u32[]{:S(2)}) collective-permute-start(f32[64,512]{1,0:T(8,128)S(1)} %get-tuple-element.48), channel_id=1, source_target_pairs={{0,8},{1,9},{2,10},{3,11},{4,12},{5,13},{6,14},{7,15},{8,0},{9,1},... | collective-permute-start | bytes 393224 | tf_op jit(solution)/shard_map/ppermute | solution.py:57
  49.7 0.8 collective-permute-start.10
  50.5 0.7 collective-permute-start.9
  51.2 2.3 %collective-permute-start.6 = (f32[224,512]{1,0:T(8,128)S(1)}, f32[224,512]{1,0:T(8,128)S(1)}, u32[]{:S(2)}, u32[]{:S(2)}) collective-permute-start(f32[224,512]{1,0:T(8,128)S(1)} %add_add_fusion.refs_0_), channel_id=1, source_target_pairs={{0,96},{16,112},{32,0},{48,16},{64,32},{80,48},{96,64},{112,80},{1... | collective-permute-start | bytes 1376264 | tf_op jit(solution)/shard_map/ppermute | solution.py:83
  53.5 0.6 collective-permute-start.5
  54.1 0.5 collective-permute-start.4
  54.6 1.5 collective-permute-done.10
  56.2 3.7 %collective-permute-start.11 = (f32[16,512]{1,0:T(8,128)S(1)}, f32[16,512]{1,0:T(8,128)S(1)}, u32[]{:S(2)}, u32[]{:S(2)}) collective-permute-start(f32[16,512]{1,0:T(8,128)S(1)} %get-tuple-element.51), channel_id=1, source_target_pairs={{0,2},{1,3},{2,0},{3,1},{4,6},{5,7},{6,4},{7,5},{8,10},{9,11},{10,... | collective-permute-start | bytes 98312 | tf_op jit(solution)/shard_map/ppermute | solution.py:57
  59.9 0.4 collective-permute-start.13
  60.3 1.2 collective-permute-done.11
  61.5 1.0 collective-permute-start.12
  62.5 0.5 collective-permute-done.13
  62.9 3.3 %collective-permute-done.12 = f32[16,512]{1,0:T(8,128)S(1)} collective-permute-done((f32[16,512]{1,0:T(8,128)S(1)}, f32[16,512]{1,0:T(8,128)S(1)}, u32[]{:S(2)}, u32[]{:S(2)}) %collective-permute-start.12) | collective-permute-done | bytes 32800 | tf_op jit(solution)/shard_map/ppermute | solution.py:57
  66.3 11.0 %collective-permute-done.4.refs_1_ = f32[224,512]{1,0:T(8,128)S(1)} collective-permute-done((f32[224,512]{1,0:T(8,128)S(1)}, f32[224,512]{1,0:T(8,128)S(1)}, u32[]{:S(2)}, u32[]{:S(2)}) %collective-permute-start.4) | collective-permute-done | bytes 458784 | tf_op jit(solution)/shard_map/ppermute | solution.py:83
  77.3 0.5 collective-permute-start.14
  77.8 0.5 collective-permute-start.16
  78.3 0.1 pad_add_fusion.place_ref
  78.4 0.3 collective-permute-start.20
  78.7 0.5 collective-permute-done.14.refs_4_
  79.2 0.6 collective-permute-start.19
  79.8 0.1 collective-permute-done.15.refs_5_
  79.9 0.3 collective-permute-start.18
  80.1 0.4 collective-permute-done.16.refs_6_
  80.5 0.7 collective-permute-done.17.refs_7_
  81.2 10.3 %blended_times_left.1 = (f32[1024,512]{1,0:T(8,128)S(1)}, f32[8,224,512]{2,1,0:T(8,128)}) custom-call(s32[2]{0:T(128)S(1)} %pad_add_fusion.place_ref, f32[1024,1792]{1,0:T(8,128)} %momentum_ref.7, bf16[1024,1792]{1,0:T(8,128)(2,1)} %gradient_ref.7, f32[224,512]{1,0:T(8,128)S(1)} %add_add_fusion.refs_0_, f32[224,512]{1,0:T(8,128)S(1)} %collective-permute-done.4.refs_1_, ...), custom_call_target="tpu_custom_call" | custom-call | flops 5637144576 | bytes 18350080 | tf_op jit(solution)/shard_map/blended_times_left/pallas_call | solution.py:249
  91.5 0.1 broadcast_in_dim.7
  91.6 0.3 pad_maximum_fusion
  91.9 39.5 %all_to_all.10 = f32[16,80,512]{2,1,0:T(8,128)} all-to-all(f32[16,80,512]{2,1,0:T(8,128)S(1)} %pad_maximum_fusion), channel_id=1, replica_groups=mesh['row'=8,'col'=16] {'col'}, dimensions={0} | all-to-all | bytes 5242880 | tf_op jit(solution)/shard_map/all_to_all | solution.py:363
  131.4 1.8 slice_reduce_fusion
  133.2 1.6 broadcast_in_dim.8
  134.8 3.7 %all-to-all-start.1 = ((f32[16,64,512]{2,1,0:T(8,128)}), f32[16,64,512]{2,1,0:T(8,128)S(1)}, u32[]{:S(2)}, u32[]{:S(2)}) async-start(f32[16,64,512]{2,1,0:T(8,128)} %broadcast_in_dim.8), calls=%async_computation.1 | async-start | bytes 4194304 | tf_op jit(solution)/shard_map/all_to_all | solution.py:363
  138.5 1.1 slice.8
  139.6 2.1 %collective-permute-start.21 = (f32[256,512]{1,0:T(8,128)S(1)}, f32[256,512]{1,0:T(8,128)S(1)}, u32[]{:S(2)}, u32[]{:S(2)}) collective-permute-start(f32[256,512]{1,0:T(8,128)S(1)} %bitcast.12), channel_id=1, source_target_pairs={{0,16},{16,0},{32,48},{48,32},{64,80},{80,64},{96,112},{112,96},{1... | collective-permute-start | bytes 1572872 | tf_op jit(solution)/shard_map/ppermute | solution.py:79
  141.8 0.1 broadcast_in_dim.6
  141.9 1.4 collective-permute-done.21
  143.4 18.4 %inverse_of_factor.1.inverse_ref = f32[512,512]{1,0:T(8,128)S(1)} custom-call(f32[512,512]{1,0:T(8,128)S(1)} %constant_dynamic-update-slice_fusion.gram_ref), custom_call_target="tpu_custom_call" | custom-call | flops 3221225472 | bytes 2097152 | tf_op jit(solution)/shard_map/inverse_of_factor/pallas_call | solution.py:134
  161.7 4.7 %ortho_halves.1 = (bf16[512,1792]{1,0:T(8,128)(2,1)S(1)}, bf16[512,1792]{1,0:T(8,128)(2,1)S(1)}) custom-call(f32[1792,512]{1,0:T(8,128)S(1)} %bitcast.11, f32[512,512]{1,0:T(8,128)S(1)} %inverse_of_factor.1.inverse_ref), custom_call_target="tpu_custom_call" | custom-call | flops 2818572288 | bytes 7340032 | tf_op jit(solution)/shard_map/ortho_halves/pallas_call | solution.py:274
  166.5 1.2 copy-done.2
  167.7 1.3 copy-done.6
  169.0 2.6 %right_and_squares.1 = (f32[1024,512]{1,0:T(8,128)S(1)}, f32[1,512]{1,0:T(1,128)S(1)}) custom-call(f32[1024,512]{1,0:T(8,128)S(1)} %bitcast.9, f32[512,512]{1,0:T(8,128)S(1)} %inverse_of_factor.1.inverse_ref), custom_call_target="tpu_custom_call" | custom-call | flops 1610612736 | bytes 4194304 | tf_op jit(solution)/shard_map/right_and_squares/pallas_call | solution.py:301
  171.6 0.5 collective-permute-start.22
  172.1 0.8 collective-permute-done.22
  172.9 1.4 collective-permute-start.25
  174.3 0.1 collective-permute-start.24
  174.4 2.3 %collective-permute-start.23 = (f32[1,512]{1,0:T(1,128)S(1)}, f32[1,512]{1,0:T(1,128)S(1)}, u32[]{:S(2)}, u32[]{:S(2)}) collective-permute-start(f32[1,512]{1,0:T(1,128)S(1)} %add.236), channel_id=1, source_target_pairs={{0,64},{16,80},{32,96},{48,112},{64,0},{80,16},{96,32},{112,48},{1... | collective-permute-start | bytes 6152 | tf_op jit(solution)/shard_map/ppermute | solution.py:52
  176.7 3.1 %copy-done = f32[1024,1792]{1,0:T(8,128)S(1)} copy-done((f32[1024,1792]{1,0:T(8,128)S(1)}, f32[1024,1792]{1,0:T(8,128)}, u32[]{:S(2)}) %copy-start) | copy-done | bytes 7340056
  179.8 4.4 %next_momentum.1 = f32[1024,1792]{1,0:T(8,128)} custom-call(f32[1024,512]{1,0:T(8,128)S(1)} %get-tuple-element.39.right_ref, bf16[512,1792]{1,0:T(8,128)(2,1)S(1)} %copy-done.3, f32[1024,1792]{1,0:T(8,128)S(1)} %copy-done, bf16[1024,1792]{1,0:T(8,128)(2,1)S(1)} %copy-done.1), custom_call_target="tpu_custom_call" | custom-call | flops 1879048192 | bytes 18350080 | tf_op jit(solution)/shard_map/next_momentum/pallas_call | solution.py:323
  184.2 0.5 copy-done.7
  184.7 7.4 %next_weight.1 = (f32[1024,512]{1,0:T(8,128)}, bf16[1024,1792]{1,0:T(8,128)(2,1)}) custom-call(f32[1024,512]{1,0:T(8,128)S(1)} %get-tuple-element.39.right_ref, f32[1,512]{1,0:T(1,128)S(1)} %add_add_fusion.4.squares_ref, bf16[512,1792]{1,0:T(8,128)(2,1)S(1)} %copy-done.3, bf16[512,1792]{1,0:T(8,128)(2,1)S(1)} %copy-done.7, bf16[1024,1792]{1,0:T(8,128)(2,1)S(1)} %copy-done.4), custom_call_target="tpu_custom_call" | custom-call | flops 5637144576 | bytes 11534336 | tf_op jit(solution)/shard_map/next_weight/pallas_call | solution.py:348
  (36 shorter events, 0.4 us)
Async XLA Ops:
  7.5 8.3 %collective-permute-start = (f32[896,512]{1,0:T(8,128)}, f32[896,512]{1,0:T(8,128)S(1)}, u32[]{:S(2)}, u32[]{:S(2)}) collective-permute-start(f32[896,512]{1,0:T(8,128)} %left_half.3), channel_id=1, source_target_pairs={{0,16},{16,0},{32,48},{48,32},{64,80},{80,64},{96,112},{112,96},{1... | collective-permute-start | bytes 5505032 | tf_op jit(solution)/shard_map/ppermute | solution.py:378
  17.4 13.9 %collective-permute-start.1 = (f32[224,512]{1,0:T(8,128)S(1)}, f32[224,512]{1,0:T(8,128)}, u32[]{:S(2)}, u32[]{:S(2)}) collective-permute-start(f32[224,512]{1,0:T(8,128)S(1)} %get-tuple-element.45), channel_id=1, source_target_pairs={{0,64},{16,80},{32,96},{48,112},{64,0},{80,16},{96,32},{112,48},{1... | collective-permute-start | bytes 1376264 | tf_op jit(solution)/shard_map/ppermute | solution.py:382
  20.3 21.0 %collective-permute-start.3 = (f32[224,512]{1,0:T(8,128)S(1)}, f32[224,512]{1,0:T(8,128)}, u32[]{:S(2)}, u32[]{:S(2)}) collective-permute-start(f32[224,512]{1,0:T(8,128)S(1)} %get-tuple-element.46), channel_id=1, source_target_pairs={{0,96},{16,112},{32,0},{48,16},{64,32},{80,48},{96,64},{112,80},{1... | collective-permute-start | bytes 1376264 | tf_op jit(solution)/shard_map/ppermute | solution.py:382
  21.2 20.2 %collective-permute-start.2 = (f32[224,512]{1,0:T(8,128)S(1)}, f32[224,512]{1,0:T(8,128)}, u32[]{:S(2)}, u32[]{:S(2)}) collective-permute-start(f32[224,512]{1,0:T(8,128)S(1)} %get-tuple-element.47), channel_id=1, source_target_pairs={{0,32},{16,48},{32,64},{48,80},{64,96},{80,112},{96,0},{112,16},{1... | collective-permute-start | bytes 1376264 | tf_op jit(solution)/shard_map/ppermute | solution.py:382
  44.2 2.4 %collective-permute-start.7 = (f32[256,512]{1,0:T(8,128)S(1)}, f32[256,512]{1,0:T(8,128)S(1)}, u32[]{:S(2)}, u32[]{:S(2)}) collective-permute-start(f32[256,512]{1,0:T(8,128)S(1)} %constant_dynamic-slice_fusion.6), channel_id=1, source_target_pairs={{0,16},{16,0},{32,48},{48,32},{64,80},{80,64},{96,112},{112,96},{1... | collective-permute-start | bytes 1572872 | tf_op jit(solution)/shard_map/ppermute | solution.py:72
  46.7 7.4 %collective-permute-start.8 = (f32[64,512]{1,0:T(8,128)S(1)}, f32[64,512]{1,0:T(8,128)S(1)}, u32[]{:S(2)}, u32[]{:S(2)}) collective-permute-start(f32[64,512]{1,0:T(8,128)S(1)} %get-tuple-element.48), channel_id=1, source_target_pairs={{0,8},{1,9},{2,10},{3,11},{4,12},{5,13},{6,14},{7,15},{8,0},{9,1},... | collective-permute-start | bytes 393224 | tf_op jit(solution)/shard_map/ppermute | solution.py:57
  49.7 6.5 %collective-permute-start.10 = (f32[64,512]{1,0:T(8,128)S(1)}, f32[64,512]{1,0:T(8,128)S(1)}, u32[]{:S(2)}, u32[]{:S(2)}) collective-permute-start(f32[64,512]{1,0:T(8,128)S(1)} %get-tuple-element.49), channel_id=1, source_target_pairs={{0,12},{1,13},{2,14},{3,15},{4,0},{5,1},{6,2},{7,3},{8,4},{9,5},{1... | collective-permute-start | bytes 393224 | tf_op jit(solution)/shard_map/ppermute | solution.py:57
  50.5 5.7 %collective-permute-start.9 = (f32[64,512]{1,0:T(8,128)S(1)}, f32[64,512]{1,0:T(8,128)S(1)}, u32[]{:S(2)}, u32[]{:S(2)}) collective-permute-start(f32[64,512]{1,0:T(8,128)S(1)} %get-tuple-element.50), channel_id=1, source_target_pairs={{0,4},{1,5},{2,6},{3,7},{4,8},{5,9},{6,10},{7,11},{8,12},{9,13},{1... | collective-permute-start | bytes 393224 | tf_op jit(solution)/shard_map/ppermute | solution.py:57
  51.2 15.1 %collective-permute-start.6 = (f32[224,512]{1,0:T(8,128)S(1)}, f32[224,512]{1,0:T(8,128)S(1)}, u32[]{:S(2)}, u32[]{:S(2)}) collective-permute-start(f32[224,512]{1,0:T(8,128)S(1)} %add_add_fusion.refs_0_), channel_id=1, source_target_pairs={{0,96},{16,112},{32,0},{48,16},{64,32},{80,48},{96,64},{112,80},{1... | collective-permute-start | bytes 1376264 | tf_op jit(solution)/shard_map/ppermute | solution.py:83
  53.5 12.7 %collective-permute-start.5 = (f32[224,512]{1,0:T(8,128)S(1)}, f32[224,512]{1,0:T(8,128)S(1)}, u32[]{:S(2)}, u32[]{:S(2)}) collective-permute-start(f32[224,512]{1,0:T(8,128)S(1)} %add_add_fusion.refs_0_), channel_id=1, source_target_pairs={{0,64},{16,80},{32,96},{48,112},{64,0},{80,16},{96,32},{112,48},{1... | collective-permute-start | bytes 1376264 | tf_op jit(solution)/shard_map/ppermute | solution.py:83
  54.1 23.2 %collective-permute-start.4 = (f32[224,512]{1,0:T(8,128)S(1)}, f32[224,512]{1,0:T(8,128)S(1)}, u32[]{:S(2)}, u32[]{:S(2)}) collective-permute-start(f32[224,512]{1,0:T(8,128)S(1)} %add_add_fusion.refs_0_), channel_id=1, source_target_pairs={{0,32},{16,48},{32,64},{48,80},{64,96},{80,112},{96,0},{112,16},{1... | collective-permute-start | bytes 1376264 | tf_op jit(solution)/shard_map/ppermute | solution.py:83
  56.2 5.3 %collective-permute-start.11 = (f32[16,512]{1,0:T(8,128)S(1)}, f32[16,512]{1,0:T(8,128)S(1)}, u32[]{:S(2)}, u32[]{:S(2)}) collective-permute-start(f32[16,512]{1,0:T(8,128)S(1)} %get-tuple-element.51), channel_id=1, source_target_pairs={{0,2},{1,3},{2,0},{3,1},{4,6},{5,7},{6,4},{7,5},{8,10},{9,11},{10,... | collective-permute-start | bytes 98312 | tf_op jit(solution)/shard_map/ppermute | solution.py:57
  59.9 3.1 %collective-permute-start.13 = (f32[16,512]{1,0:T(8,128)S(1)}, f32[16,512]{1,0:T(8,128)S(1)}, u32[]{:S(2)}, u32[]{:S(2)}) collective-permute-start(f32[16,512]{1,0:T(8,128)S(1)} %get-tuple-element.52), channel_id=1, source_target_pairs={{0,3},{1,0},{2,1},{3,2},{4,7},{5,4},{6,5},{7,6},{8,11},{9,8},{10,9... | collective-permute-start | bytes 98312 | tf_op jit(solution)/shard_map/ppermute | solution.py:57
  61.5 4.8 %collective-permute-start.12 = (f32[16,512]{1,0:T(8,128)S(1)}, f32[16,512]{1,0:T(8,128)S(1)}, u32[]{:S(2)}, u32[]{:S(2)}) collective-permute-start(f32[16,512]{1,0:T(8,128)S(1)} %get-tuple-element.53), channel_id=1, source_target_pairs={{0,1},{1,2},{2,3},{3,0},{4,5},{5,6},{6,7},{7,4},{8,9},{9,10},{10,1... | collective-permute-start | bytes 98312 | tf_op jit(solution)/shard_map/ppermute | solution.py:57
  77.3 1.9 %collective-permute-start.14 = (f32[224,512]{1,0:T(8,128)S(1)}, f32[224,512]{1,0:T(8,128)S(1)}, u32[]{:S(2)}, u32[]{:S(2)}) collective-permute-start(f32[224,512]{1,0:T(8,128)S(1)} %add_add_fusion.refs_0_), channel_id=1, source_target_pairs={{0,16},{16,0},{32,48},{48,32},{64,80},{80,64},{96,112},{112,96},{1... | collective-permute-start | bytes 1376264 | tf_op jit(solution)/shard_map/ppermute | solution.py:388
  77.8 2.1 %collective-permute-start.15 = (f32[224,512]{1,0:T(8,128)S(1)}, f32[224,512]{1,0:T(8,128)S(1)}, u32[]{:S(2)}, u32[]{:S(2)}) collective-permute-start(f32[224,512]{1,0:T(8,128)S(1)} %collective-permute-done.4.refs_1_), channel_id=1, source_target_pairs={{0,16},{16,0},{32,48},{48,32},{64,80},{80,64},{96,112},{112,96},{1... | collective-permute-start | bytes 1376264 | tf_op jit(solution)/shard_map/ppermute | solution.py:388
  77.8 2.7 %collective-permute-start.16 = (f32[224,512]{1,0:T(8,128)S(1)}, f32[224,512]{1,0:T(8,128)S(1)}, u32[]{:S(2)}, u32[]{:S(2)}) collective-permute-start(f32[224,512]{1,0:T(8,128)S(1)} %collective-permute-done.5.refs_2_), channel_id=1, source_target_pairs={{0,16},{16,0},{32,48},{48,32},{64,80},{80,64},{96,112},{112,96},{1... | collective-permute-start | bytes 1376264 | tf_op jit(solution)/shard_map/ppermute | solution.py:388
  78.3 2.9 %collective-permute-start.17 = (f32[224,512]{1,0:T(8,128)S(1)}, f32[224,512]{1,0:T(8,128)S(1)}, u32[]{:S(2)}, u32[]{:S(2)}) collective-permute-start(f32[224,512]{1,0:T(8,128)S(1)} %collective-permute-done.6.refs_3_), channel_id=1, source_target_pairs={{0,16},{16,0},{32,48},{48,32},{64,80},{80,64},{96,112},{112,96},{1... | collective-permute-start | bytes 1376264 | tf_op jit(solution)/shard_map/ppermute | solution.py:388
  78.4 13.1 %collective-permute-start.20 = (f32[16,512]{1,0:T(8,128)S(1)}, f32[16,512]{1,0:T(8,128)S(1)}, u32[]{:S(2)}, u32[]{:S(2)}) collective-permute-start(f32[16,512]{1,0:T(8,128)S(1)} %add_add_fusion.3), channel_id=1, source_target_pairs={{0,96},{16,112},{32,0},{48,16},{64,32},{80,48},{96,64},{112,80},{1... | collective-permute-start | bytes 98312 | tf_op jit(solution)/shard_map/ppermute | solution.py:83
  79.2 12.3 %collective-permute-start.19 = (f32[16,512]{1,0:T(8,128)S(1)}, f32[16,512]{1,0:T(8,128)S(1)}, u32[]{:S(2)}, u32[]{:S(2)}) collective-permute-start(f32[16,512]{1,0:T(8,128)S(1)} %add_add_fusion.3), channel_id=1, source_target_pairs={{0,64},{16,80},{32,96},{48,112},{64,0},{80,16},{96,32},{112,48},{1... | collective-permute-start | bytes 98312 | tf_op jit(solution)/shard_map/ppermute | solution.py:83
  79.9 11.6 %collective-permute-start.18 = (f32[16,512]{1,0:T(8,128)S(1)}, f32[16,512]{1,0:T(8,128)S(1)}, u32[]{:S(2)}, u32[]{:S(2)}) collective-permute-start(f32[16,512]{1,0:T(8,128)S(1)} %add_add_fusion.3), channel_id=1, source_target_pairs={{0,32},{16,48},{32,64},{48,80},{64,96},{80,112},{96,0},{112,16},{1... | collective-permute-start | bytes 98312 | tf_op jit(solution)/shard_map/ppermute | solution.py:83
  134.8 34.2 %all-to-all-start.1 = ((f32[16,64,512]{2,1,0:T(8,128)}), f32[16,64,512]{2,1,0:T(8,128)S(1)}, u32[]{:S(2)}, u32[]{:S(2)}) async-start(f32[16,64,512]{2,1,0:T(8,128)} %broadcast_in_dim.8), calls=%async_computation.1 | async-start | bytes 4194304 | tf_op jit(solution)/shard_map/all_to_all | solution.py:363
  139.6 3.7 %collective-permute-start.21 = (f32[256,512]{1,0:T(8,128)S(1)}, f32[256,512]{1,0:T(8,128)S(1)}, u32[]{:S(2)}, u32[]{:S(2)}) collective-permute-start(f32[256,512]{1,0:T(8,128)S(1)} %bitcast.12), channel_id=1, source_target_pairs={{0,16},{16,0},{32,48},{48,32},{64,80},{80,64},{96,112},{112,96},{1... | collective-permute-start | bytes 1572872 | tf_op jit(solution)/shard_map/ppermute | solution.py:79
  143.3 18.4 %copy-start.5 = (f32[8,224,512]{2,1,0:T(8,128)S(1)}, f32[8,224,512]{2,1,0:T(8,128)}, u32[]{:S(2)}) copy-start(f32[8,224,512]{2,1,0:T(8,128)} %get-tuple-element.28) | copy-start | bytes 11010052
  166.5 1.2 copy-start.2
  167.7 1.3 copy-start.6
  169.0 7.7 %copy-start.1 = (bf16[1024,1792]{1,0:T(8,128)(2,1)S(1)}, bf16[1024,1792]{1,0:T(8,128)(2,1)}, u32[]{:S(2)}) copy-start(bf16[1024,1792]{1,0:T(8,128)(2,1)} %gradient_ref.7) | copy-start | bytes 11010052
  169.0 7.7 %copy-start.3 = (bf16[512,1792]{1,0:T(8,128)(2,1)S(1)}, bf16[512,1792]{1,0:T(8,128)(2,1)}, u32[]{:S(2)}) copy-start(bf16[512,1792]{1,0:T(8,128)(2,1)} %copy-done.2) | copy-start | bytes 5505028
  171.6 1.3 collective-permute-start.22
  172.9 11.2 %collective-permute-start.25 = (f32[1,512]{1,0:T(1,128)S(1)}, f32[1,512]{1,0:T(1,128)S(1)}, u32[]{:S(2)}, u32[]{:S(2)}) collective-permute-start(f32[1,512]{1,0:T(1,128)S(1)} %add.236), channel_id=1, source_target_pairs={{0,96},{16,112},{32,0},{48,16},{64,32},{80,48},{96,64},{112,80},{1... | collective-permute-start | bytes 6152 | tf_op jit(solution)/shard_map/ppermute | solution.py:52
  174.3 9.9 %collective-permute-start.24 = (f32[1,512]{1,0:T(1,128)S(1)}, f32[1,512]{1,0:T(1,128)S(1)}, u32[]{:S(2)}, u32[]{:S(2)}) collective-permute-start(f32[1,512]{1,0:T(1,128)S(1)} %add.236), channel_id=1, source_target_pairs={{0,32},{16,48},{32,64},{48,80},{64,96},{80,112},{96,0},{112,16},{1... | collective-permute-start | bytes 6152 | tf_op jit(solution)/shard_map/ppermute | solution.py:52
  174.4 9.8 %collective-permute-start.23 = (f32[1,512]{1,0:T(1,128)S(1)}, f32[1,512]{1,0:T(1,128)S(1)}, u32[]{:S(2)}, u32[]{:S(2)}) collective-permute-start(f32[1,512]{1,0:T(1,128)S(1)} %add.236), channel_id=1, source_target_pairs={{0,64},{16,80},{32,96},{48,112},{64,0},{80,16},{96,32},{112,48},{1... | collective-permute-start | bytes 6152 | tf_op jit(solution)/shard_map/ppermute | solution.py:52
  176.7 3.1 %copy-start = (f32[1024,1792]{1,0:T(8,128)S(1)}, f32[1024,1792]{1,0:T(8,128)}, u32[]{:S(2)}) copy-start(f32[1024,1792]{1,0:T(8,128)} %momentum_ref.7) | copy-start | bytes 22020100
  179.7 4.5 %copy-start.4 = (bf16[1024,1792]{1,0:T(8,128)(2,1)S(1)}, bf16[1024,1792]{1,0:T(8,128)(2,1)}, u32[]{:S(2)}) copy-start(bf16[1024,1792]{1,0:T(8,128)(2,1)} %weight_ref.1) | copy-start | bytes 11010052
  179.8 4.9 %copy-start.7 = (bf16[512,1792]{1,0:T(8,128)(2,1)S(1)}, bf16[512,1792]{1,0:T(8,128)(2,1)}, u32[]{:S(2)}) copy-start(bf16[512,1792]{1,0:T(8,128)(2,1)} %copy-done.6) | copy-start | bytes 5505028
